TPU v7x, 32 devices: a whole 2x2x4 slice. The times are simulated.
32 devices in a mesh: dp: 32 (over z, y, x, core).
Axes of the slice: x: 2, y: 2, z: 4, core: 2. Of those that a mesh axis runs over, the one named last changes fastest.
Arguments:
- tokens: bfloat16 [32, 1024, 768], P('dp'), may hold values from -6 to 6
- image_features: bfloat16 [32, 1024, 768], P('dp'), may hold values from -3 to 3
- segment_ids: int32 [32, 1024], P('dp'), may hold values from 0 to 7, never falling along the last dimension, each value on 1 to 512 neighbouring positions
- box_left: int32 [32, 1024], P('dp'), may hold values from 0 to 255
- box_top: int32 [32, 1024], P('dp'), may hold values from 0 to 255
- cotangent: bfloat16 [32, 1024, 768], P('dp'), may hold values from -6 to 6
- query_weight: bfloat16 [768, 768], P('dp'), may hold values from -0.21875 to 0.21875
- key_weight: bfloat16 [768, 768], P('dp'), may hold values from -0.21875 to 0.21875
- value_weight: bfloat16 [768, 768], P('dp'), may hold values from -0.21875 to 0.21875
- output_weight: bfloat16 [768, 768], P('dp'), may hold values from -0.625 to 0.625
- inner_weight: bfloat16 [768, 3072], P('dp'), may hold values from -0.21875 to 0.21875
- outer_weight: bfloat16 [3072, 768], P('dp'), may hold values from -0.109375 to 0.109375
- attention_gain: bfloat16 [768], P('dp'), may hold values from 0.25 to 1.75
- feed_gain: bfloat16 [768], P('dp'), may hold values from 0.25 to 1.75
- bias_tables: bfloat16 [1152], P('dp'), may hold values from -3 to 3
Outputs:
- layer_output: bfloat16 [32, 1024, 768], P('dp')
- input_gradient: float32 [32, 1024, 768], P('dp')
- query_gradient: float32 [768, 768], P('dp')
- key_gradient: float32 [768, 768], P('dp')
- value_gradient: float32 [768, 768], P('dp')
- projection_gradient: float32 [768, 768], P('dp')
- inner_gradient: float32 [768, 3072], P('dp')
- outer_gradient: float32 [3072, 768], P('dp')
- attention_gain_gradient: float32 [768], P('dp')
- feed_gain_gradient: float32 [768], P('dp')
- tables_gradient: float32 [1152], P('dp')
Inputs may be any that keep to these rules, and one draw needn't show every extreme that they name: `segment_ids`: per row, never falling; each document has 1 to 512 tokens and one has exactly that many.
All inputs are finite; a program needn't handle non-finite values.
Results may differ from a plain program's by a relative error of at most 0.013.
Values may be sent and summed in bfloat16 or wider, within the bound.
No kernel may reach another device: no remote copies, remote signals or barrier semaphores. Data moves between devices by JAX's collectives and lax.ppermute only.
A program may use at most 384 MiB of HBM per device.

v0:
```python
import functools

import numpy as np
import jax
import jax.numpy as jnp
from jax import lax
from jax.sharding import PartitionSpec as P
from jax.experimental import pallas as pl
from jax.experimental.pallas import tpu as pltpu

HEADS = 12
BUCKETS = 32
thresholds = (1, 2, 3, 4, 5, 6, 7, 8, 11, 16, 22, 32, 45, 64, 90)
COORDS = 256
TILE = 256
LANES = 128
AHEAD = 3
SMALL = pl.CostEstimate(flops=10**8, bytes_accessed=10**5, transcendentals=0)
F32 = jnp.float32
BF16 = jnp.bfloat16
NT = (((1,), (1,)), ((), ()))
NN = (((1,), (0,)), ((), ()))
TN = (((0,), (0,)), ((), ()))


def bucket_of(offset):
    magnitude = np.zeros(offset.shape, np.int32)
    for limit in thresholds:
        magnitude = magnitude + (np.abs(offset) >= limit).astype(np.int32)
    return magnitude + BUCKETS // 2 * (offset > 0).astype(np.int32)


def dot(left, right, dims=NN):
    return lax.dot_general(left, right, dims, preferred_element_type=F32)


def rows_of(tables):
    spot = np.arange(2 * TILE)
    signed = np.where(spot < TILE, spot, spot - 2 * TILE)
    marks = np.zeros((3, BUCKETS, 8, 2 * TILE), np.float32)
    picks = ((1, -signed), (2, -signed), (0, -signed), (0, TILE - signed), (0, -TILE - signed))
    for place, (table_index, offset) in enumerate(picks):
        marks[table_index, bucket_of(offset), place, spot] = 1.0
    marks = marks.reshape(3 * BUCKETS, 16 * TILE).astype(BF16)
    return dot(tables, jnp.asarray(marks), TN).reshape(HEADS, 8, 2 * TILE)


def bucket_marks():
    spot = np.arange(2 * TILE)
    falling = TILE - 1 - spot
    rising = spot - (TILE - 1)
    offsets = np.stack([falling, falling, rising, TILE + rising, rising - TILE], axis=1)
    marks = bucket_of(offsets)[:, :, None] == np.arange(LANES)
    return jnp.asarray(marks.astype(BF16).reshape(2 * TILE, 5 * LANES))


def toeplitz(row):
    wide = jnp.broadcast_to(row, (TILE, 2 * TILE))
    return pltpu.roll(wide, 0, axis=1, stride=1, stride_axis=0)[:, :TILE]


def skew_sum(square):
    wide = jnp.concatenate([square, jnp.zeros_like(square)], axis=1)
    return jnp.sum(pltpu.roll(wide, 0, axis=1, stride=1, stride_axis=0), axis=0, keepdims=True)


def one_hot_lanes(column, width):
    return (column == lax.broadcasted_iota(jnp.int32, (column.shape[0], width), 1)).astype(F32).astype(BF16)


def attend_kernel(qkv_ref, band_ref, seg_ref, seg_row, left_ref, top_ref, left_row, top_row, out_ref, probs_ref, sums_ref,
                key_side, query_side, position, marks):
    length = qkv_ref.shape[0]
    half = length // 2

    @pl.when(pl.program_id(0) == 0)
    def _():
        key_side[:, LANES:2 * LANES] = one_hot_lanes(seg_ref[...], LANES)
        key_side[:, 2 * LANES:2 * LANES + COORDS] = one_hot_lanes(left_ref[...], COORDS)
        key_side[:, 2 * LANES + COORDS:] = one_hot_lanes(top_ref[...], COORDS)
        down = lax.broadcasted_iota(jnp.int32, (LANES, length), 0)
        other = jnp.where(jnp.logical_and(down < 8, down != seg_row[...]), F32(-1e30), F32(0)).astype(BF16)
        query_side[0, LANES:2 * LANES, :] = other
        query_side[1, LANES:2 * LANES, :] = other
        down = lax.broadcasted_iota(jnp.int32, (COORDS, length), 0)
        marks[0] = (down == left_row[...]).astype(F32).astype(BF16)
        marks[1] = (down == top_row[...]).astype(F32).astype(BF16)
        query_side[0, 64:LANES, :] = jnp.zeros((64, length), BF16)
        query_side[1, :64, :] = jnp.zeros((64, length), BF16)

    key_side[:, :LANES] = qkv_ref[:, LANES:2 * LANES]
    values_across = qkv_ref[:, 2 * LANES:].T
    queries_across = qkv_ref[:, :LANES].T
    for h in range(2):
        bands = band_ref[h]
        own = slice(h * 64, (h + 1) * 64)
        query_side[h, own, :] = queries_across[own]
        middle, below, above = (toeplitz(bands[t:t + 1]) for t in (2, 3, 4))
        position[h, :TILE, :TILE] = middle
        position[h, TILE:, TILE:] = middle
        position[h, TILE:, :TILE] = below
        position[h, :TILE, TILE:] = above

    for t in range(2):
        low = 2 * LANES + t * COORDS
        grids = jnp.concatenate([toeplitz(band_ref[h, t:t + 1]) for h in range(2)], axis=0).astype(BF16)
        spread = dot(grids, marks[t]).astype(BF16)
        for h in range(2):
            query_side[h, low:low + COORDS, :] = spread[h * COORDS:(h + 1) * COORDS]

    def logits_of(block, tile, h):
        rows = slice(block * half, (block + 1) * half)
        here = slice(block * half + tile * TILE, block * half + (tile + 1) * TILE)
        return dot(key_side[rows, :], query_side[h, :, here]) + position[h, :, tile * TILE:(tile + 1) * TILE]

    def finish(block, tile, h, logits):
        rows = slice(block * half, (block + 1) * half)
        across = slice(tile * TILE, (tile + 1) * TILE)
        here = slice(block * half + tile * TILE, block * half + (tile + 1) * TILE)
        raised = jnp.exp(logits - jnp.max(logits, axis=0, keepdims=True))
        inverse = 1.0 / jnp.sum(raised, axis=0, keepdims=True)
        low = raised.astype(BF16)
        probs_ref[h, rows, across] = low
        sums_ref[h, :, here] = inverse
        return dot(values_across[h * 64:(h + 1) * 64, rows], low) * inverse

    jobs = [(block, tile, h) for block in range(2) for tile in range(half // TILE) for h in range(2)]
    pieces = {}

    def close(job, logits):
        block, tile, h = job
        pieces[job] = finish(*job, logits)
        if h == 1:
            here = slice(block * half + tile * TILE, block * half + (tile + 1) * TILE)
            out_ref[here, :] = jnp.concatenate([pieces[(block, tile, 0)], pieces[(block, tile, 1)]], axis=0).T.astype(BF16)

    waiting = []
    for job in jobs:
        waiting.append((job, logits_of(*job)))
        if len(waiting) > AHEAD:
            close(*waiting.pop(0))
    for item in waiting:
        close(*item)


def attend(packed, bands, seg, left, top, columns):
    length, width = packed.shape[0], packed.shape[1] // 3
    pair = pl.BlockSpec((length, LANES), lambda g: (0, g))
    column = pl.BlockSpec((length, 1), lambda g: (0, 0))
    row = pl.BlockSpec((1, length), lambda g: (0, 0))
    return pl.pallas_call(
        attend_kernel,
        grid=(HEADS // 2,),
        in_specs=[
            pl.BlockSpec((length, 3 * LANES), lambda g: (0, g)),
            pl.BlockSpec((2, 8, 2 * TILE), lambda g: (g, 0, 0)),
            column, row, column, column, row, row,
        ],
        out_specs=[pair, pl.BlockSpec((2, length, length // 2), lambda g: (g, 0, 0)), pl.BlockSpec((2, 1, length), lambda g: (g, 0, 0))],
        out_shape=[
            jax.ShapeDtypeStruct((length, width), BF16),
            jax.ShapeDtypeStruct((HEADS, length, length // 2), BF16),
            jax.ShapeDtypeStruct((HEADS, 1, length), F32),
        ],
        scratch_shapes=[
            pltpu.VMEM((length, 2 * LANES + 2 * COORDS), BF16),
            pltpu.VMEM((2, 2 * LANES + 2 * COORDS, length), BF16),
            pltpu.VMEM((2, length // 2, length // 2), F32),
            pltpu.VMEM((2, COORDS, length), BF16),
        ],
        compiler_params=pltpu.CompilerParams(vmem_limit_bytes=58 * 1024 * 1024),
        cost_estimate=SMALL,
        name="attend",
    )(packed, bands, columns[0], seg[None], columns[1], columns[2], left[None], top[None])


def attend_back_kernel(first, qkv_ref, g_ref, probs_ref, inverse_ref, delta_ref, left_ref, top_ref, left_row, top_row, normed_ref,
                       bucket_ref, *rest):
    grad_ref, weight_ref, band_ref, key_across, marks, low_grads, spread, flip, normed_across, line_sums = rest[-10:]
    length = g_ref.shape[0]
    half = length // 2
    step = pl.program_id(0)

    @pl.when(step == 0)
    def _():
        normed_across[...] = normed_ref[...].T
        marks[:, :COORDS] = one_hot_lanes(left_ref[...], COORDS)
        marks[:, COORDS:] = one_hot_lanes(top_ref[...], COORDS)
        down = COORDS - 1 - lax.broadcasted_iota(jnp.int32, (COORDS, length), 0)
        left_marks = (down == left_row[...]).astype(F32).astype(BF16)
        top_marks = (down == top_row[...]).astype(F32).astype(BF16)
        for h in range(2):
            key_across[h, 64:64 + COORDS, :] = left_marks
            key_across[h, 64 + COORDS:, :] = top_marks
        turned = TILE - 1 - lax.broadcasted_iota(jnp.int32, (TILE, TILE), 0)
        flip[...] = (turned == lax.broadcasted_iota(jnp.int32, (TILE, TILE), 1)).astype(F32).astype(BF16)

    keys_t = qkv_ref[:, LANES:2 * LANES].T
    upper = lax.broadcasted_iota(jnp.int32, (length, LANES), 1) >= LANES // 2
    zero = jnp.zeros((), BF16)
    inverse = jnp.concatenate([inverse_ref[0], inverse_ref[1], jnp.zeros((6, length), F32)], axis=0).T
    grads_h, across_h, queries_h, delta_h = [], [], [], []
    for h in range(2):
        key_across[h, :64, :] = keys_t[h * 64:(h + 1) * 64]
        own = upper == (h == 1)
        mine = jnp.where(own, g_ref[...].astype(F32) * inverse[:, h:h + 1], 0.0).astype(BF16)
        grads_h.append(mine)
        across_h.append(mine.T)
        queries_h.append(jnp.where(own, qkv_ref[:, :LANES], zero))
        delta_h.append(delta_ref[pl.ds(2 * (first + step) + h, 1), :] * inverse_ref[h])
    values = qkv_ref[:, 2 * LANES:]

    def lanes(kind):
        return pl.ds(pl.multiple_of((step % 2) * 3 * LANES + kind * LANES, LANES), LANES)

    def spots(job):
        block, tile, h = job
        return (
            slice(block * half, (block + 1) * half),
            slice(block * half + tile * TILE, block * half + (tile + 1) * TILE),
            slice(tile * TILE, (tile + 1) * TILE),
        )

    def reach_of(job):
        rows, here, _ = spots(job)
        return dot(values[rows], across_h[job[2]][:, here])

    def push(job, reach):
        rows, here, across = spots(job)
        h = job[2]
        grads = (probs_ref[h, rows, across].astype(F32) * (reach - delta_h[h][:, here])).astype(BF16)
        low_grads[h, rows, across] = grads
        return dot(key_across[h, :, rows], grads)

    halves = {}

    def settle(job, both):
        block, tile, h = job
        rows, here, _ = spots(job)
        halves[job] = both[:64] * 0.125
        for t in range(2):
            spread[t, h * COORDS:(h + 1) * COORDS, here] = both[64 + t * COORDS:64 + (t + 1) * COORDS].astype(BF16)
        if h == 1:
            grad_ref[here, lanes(0)] = jnp.concatenate([halves[(block, tile, 0)], halves[job]], axis=0).T.astype(BF16)
        if h == 1 and tile == half // TILE - 1:
            grad_ref[rows, lanes(2)] = (
                dot(probs_ref[0, rows, :], grads_h[0][rows]) + dot(probs_ref[1, rows, :], grads_h[1][rows])
            ).astype(BF16)
            grad_ref[rows, lanes(1)] = (
                dot(low_grads[0, rows, :], queries_h[0][rows]) + dot(low_grads[1, rows, :], queries_h[1][rows])
            ).astype(BF16)

    jobs = [(block, tile, h) for block in range(2) for tile in range(half // TILE) for h in range(2)]
    reaching, pushed = [], []
    for job in jobs + [None] * 3:
        if job is not None:
            reaching.append((job, reach_of(job)))
        if reaching and (job is None or len(reaching) > 1):
            own, reach = reaching.pop(0)
            pushed.append((own, push(own, reach)))
        if pushed and (not reaching or len(pushed) > 1):
            settle(*pushed.pop(0))
    while reaching:
        own, reach = reaching.pop(0)
        pushed.append((own, push(own, reach)))
    while pushed:
        settle(*pushed.pop(0))

    @pl.when(step % 2 == 1)
    def _():
        weight_ref[...] = dot(normed_across[...], grad_ref[...]).astype(BF16)


    def part(h, block, down, tile):
        return low_grads[h, block * half + down * TILE:block * half + (down + 1) * TILE, tile * TILE:(tile + 1) * TILE].astype(F32)

    pressed = [dot(spread[t], marks[:, t * COORDS:(t + 1) * COORDS]) for t in range(2)]
    highs, rests = [], []
    for h in range(2):
        for square in (
            (part(h, 0, 0, 0) + part(h, 0, 1, 1)) + (part(h, 1, 0, 0) + part(h, 1, 1, 1)),
            part(h, 0, 1, 0) + part(h, 1, 1, 0),
            part(h, 0, 0, 1) + part(h, 1, 0, 1),
        ):
            high = square.astype(BF16)
            highs.append(high)
            rests.append((square - high.astype(F32)).astype(BF16))
    turned = dot(jnp.concatenate(highs + rests, axis=0), flip[...])
    for h in range(2):
        squares = [item[h * COORDS:(h + 1) * COORDS] for item in pressed]
        for place in range(3 * h, 3 * h + 3):
            squares.append(turned[place * TILE:(place + 1) * TILE] + turned[(place + 6) * TILE:(place + 7) * TILE])
        sums = [skew_sum(square) for square in squares]
        line_sums[pl.ds(pl.multiple_of((2 * step + h) * 8, 8), 8), :] = jnp.concatenate(
            sums + [jnp.zeros_like(sums[0])] * 3, axis=0
        )

    @pl.when(step == pl.num_programs(0) - 1)
    def _():
        lines = line_sums[...]
        count = lines.shape[0]
        high = lines.astype(BF16)
        both = dot(jnp.concatenate([high, (lines - high.astype(F32)).astype(BF16)], axis=0), bucket_ref[...])
        both = both[:count] + both[count:]
        for head in range(count // 8):
            picked = [both[head * 8 + t:head * 8 + t + 1, t * LANES:(t + 1) * LANES] for t in range(5)]
            band_ref[head] = jnp.concatenate(
                [picked[2] + picked[3] + picked[4], picked[0], picked[1], jnp.zeros((5, LANES), F32)], axis=0
            )


def attend_back(first, count, packed, grad_attended, probs, inverse, delta, left, top, columns, normed, buckets, *deps):
    length, width = grad_attended.shape
    column = pl.BlockSpec((length, 1), lambda g: (0, 0))
    row = pl.BlockSpec((1, length), lambda g: (0, 0))
    return pl.pallas_call(
        functools.partial(attend_back_kernel, first),
        grid=(count,),
        in_specs=[
            pl.BlockSpec((length, 3 * LANES), lambda g: (0, first + g)),
            pl.BlockSpec((length, LANES), lambda g: (0, first + g)),
            pl.BlockSpec((2, length, length // 2), lambda g: (first + g, 0, 0)),
            pl.BlockSpec((2, 1, length), lambda g: (first + g, 0, 0)),
            pl.BlockSpec(delta.shape, lambda g: (0, 0)),
            column, column, row, row,
            pl.BlockSpec((length, width), lambda g: (0, 0)),
            pl.BlockSpec(buckets.shape, lambda g: (0, 0)),
        ] + [pl.BlockSpec(memory_space=pl.ANY)] * len(deps),
        out_specs=[
            pl.BlockSpec((length, 6 * LANES), lambda g: (0, g // 2)),
            pl.BlockSpec((width, 6 * LANES), lambda g: (0, g // 2)),
            pl.BlockSpec((2 * count, 8, LANES), lambda g: (0, 0, 0)),
        ],
        out_shape=[
            jax.ShapeDtypeStruct((length, 3 * LANES * count), BF16),
            jax.ShapeDtypeStruct((width, 3 * LANES * count), BF16),
            jax.ShapeDtypeStruct((2 * count, 8, LANES), F32),
        ],
        scratch_shapes=[
            pltpu.VMEM((2, 64 + 2 * COORDS, length), BF16),
            pltpu.VMEM((length, 2 * COORDS), BF16),
            pltpu.VMEM((2, length, length // 2), BF16),
            pltpu.VMEM((2, 2 * COORDS, length), BF16),
            pltpu.VMEM((TILE, TILE), BF16),
            pltpu.VMEM((width, length), BF16),
            pltpu.VMEM((16 * count, 2 * TILE), F32),
        ],
        compiler_params=pltpu.CompilerParams(vmem_limit_bytes=58 * 1024 * 1024),
        cost_estimate=SMALL,
        name="attend_back",
    )(packed, grad_attended, probs, inverse, delta, columns[1], columns[2], left[None], top[None], normed, buckets, *deps)


ROOT = float(np.sqrt(2.0 / np.pi))


def feed_kernel(width, steps, kept, att_ref, start_ref, up_ref, inner_ref, outer_ref, output_ref, gain_ref,
                middle_ref, act_ref, back_ref, early_ref, late_ref, active, inner_back, normed, upstream):
    step = pl.program_id(0)
    parts = inner_ref.shape[1] // width

    @pl.when(step < steps)
    def _():
        size = att_ref.shape[0]
        rows = pl.ds(pl.multiple_of(step * size, size), size)
        up = up_ref[...]
        upstream[rows, :] = up
        middle = start_ref[...] + dot(att_ref[...], output_ref[...])
        middle_ref[...] = middle
        root = lax.rsqrt(jnp.mean(middle * middle, axis=1, keepdims=True) + 1e-06)
        low = (middle * root * gain_ref[...]).astype(BF16)
        normed[rows, :] = low

        def products(part):
            own = slice(part * width, (part + 1) * width)
            return dot(low, inner_ref[:, own]), dot(up, outer_ref[:, own], NT)

        def finish(part, point, reach):
            own = slice(part * width, (part + 1) * width)
            square = point * point
            bend = jnp.tanh(ROOT * point * (1.0 + 0.044715 * square))
            half = 0.5 + 0.5 * bend
            act = (point * half).astype(BF16)
            slope = half + (0.5 * ROOT) * point * (1.0 - bend * bend) * (1.0 + (3 * 0.044715) * square)
            grads = (slope * reach).astype(BF16)
            act_ref[:, own] = act
            back_ref[:, own] = grads
            active[rows, own] = act
            inner_back[rows, own] = grads

        held = products(0)
        for part in range(1, parts):
            following = products(part)
            finish(part - 1, *held)
            held = following
        finish(parts - 1, *held)

    @pl.when(jnp.logical_and(step >= steps, step < steps + parts))
    def _():
        own = pl.ds(pl.multiple_of((step - steps) * width, width), width)
        early_ref[...] = dot(active[:, own], upstream[...], TN).astype(BF16)

    def inner_grad():
        own = pl.ds(pl.multiple_of((step - steps - parts) * width, width), width)
        return dot(normed[...], inner_back[:, own], TN).astype(BF16)

    @pl.when(jnp.logical_and(step >= steps + parts, step < steps + parts + kept))
    def _():
        early_ref[...] = inner_grad()

    @pl.when(step >= steps + parts + kept)
    def _():
        late_ref[...] = inner_grad()


def weight_specs(width, parts, places):
    once = pl.Buffered(1)
    specs = [
        pl.BlockSpec((width, parts * width), lambda g: (0, 0), pipeline_mode=once),
        pl.BlockSpec((width, parts * width), lambda g: (0, 1), pipeline_mode=once),
        pl.BlockSpec((width, width), lambda g: (0, 2 * parts), pipeline_mode=once),
        pl.BlockSpec((1, width), lambda g: (0, 0)),
    ]
    return [specs[place] for place in places]


def feed(kept, attended, start, upstream, weights, gain):
    length, width = attended.shape
    steps = length // TILE
    parts = weights.shape[1] // width // 2
    rows = lambda g: (jnp.minimum(g, steps - 1), 0)
    tile = pl.BlockSpec((TILE, width), rows)
    broad = pl.BlockSpec((TILE, parts * width), rows)
    return pl.pallas_call(
        functools.partial(feed_kernel, width, steps, kept),
        grid=(steps + 2 * parts,),
        in_specs=[tile, tile, tile] + weight_specs(width, parts, (0, 1, 2, 3)),
        out_specs=[
            tile, broad, broad,
            pl.BlockSpec((width, width), lambda g: (0, jnp.clip(g - steps, 0, parts + kept - 1))),
            pl.BlockSpec((width, width), lambda g: (0, jnp.maximum(g - steps - parts - kept, 0))),
        ],
        out_shape=[
            jax.ShapeDtypeStruct((length, width), F32),
            jax.ShapeDtypeStruct((length, parts * width), BF16),
            jax.ShapeDtypeStruct((length, parts * width), BF16),
            jax.ShapeDtypeStruct((width, (parts + kept) * width), BF16),
            jax.ShapeDtypeStruct((width, (parts - kept) * width), BF16),
        ],
        scratch_shapes=[pltpu.VMEM((length, parts * width), BF16)] * 2 + [pltpu.VMEM((length, width), BF16)] * 2,
        compiler_params=pltpu.CompilerParams(vmem_limit_bytes=58 * 1024 * 1024),
        cost_estimate=SMALL,
        name="feed",
    )(attended, start, upstream, weights, weights, weights, gain)


def feed_back_kernel(width, steps, att_ref, middle_ref, up_ref, act_ref, back_ref, inner_ref, outer_ref, output_ref, gain_ref,
                     *rest):
    layer_ref, out_ref, seen_ref, delta_ref, weight_ref, low_middle, attended = rest[-7:]
    step = pl.program_id(0)

    @pl.when(step < steps)
    def _():
        size = att_ref.shape[0]
        rows = pl.ds(pl.multiple_of(step * size, size), size)
        att = att_ref[...]
        attended[rows, :] = att
        gain = gain_ref[...]
        middle = middle_ref[...]
        back = dot(back_ref[...], inner_ref[...], NT)
        result = middle
        for part in range(act_ref.shape[1] // width):
            own = slice(part * width, (part + 1) * width)
            result = result + dot(act_ref[:, own], outer_ref[:, own])
        root = lax.rsqrt(jnp.mean(middle * middle, axis=1, keepdims=True) + 1e-06)
        scaled = middle * root
        slant = jnp.mean(back * scaled * gain, axis=1, keepdims=True)
        grad_middle = up_ref[...].astype(F32) + root * (gain * back - scaled * slant)
        out_ref[...] = grad_middle
        rounded = grad_middle.astype(BF16)
        low_middle[rows, :] = rounded
        layer_ref[...] = result.astype(BF16)
        seen = dot(rounded, output_ref[...], NT).astype(BF16)
        seen_ref[...] = seen
        product = att.astype(F32) * seen.astype(F32)
        high = product.astype(BF16)
        low = (product - high.astype(F32)).astype(BF16)
        head = lax.broadcasted_iota(jnp.int32, (16, width), 0)
        lane = lax.broadcasted_iota(jnp.int32, (16, width), 1)
        marks = jnp.logical_and(lane >= head * 64, lane < head * 64 + 64).astype(F32).astype(BF16)
        delta_ref[...] = dot(marks, high, NT) + dot(marks, low, NT)

    @pl.when(step == steps)
    def _():
        weight_ref[...] = dot(attended[...], low_middle[...], TN).astype(BF16)


def feed_back(attended, middle, upstream, act, back, weights, gain, *deps):
    length, width = attended.shape
    steps = length // TILE
    parts = weights.shape[1] // width // 2
    rows = lambda g: (jnp.minimum(g, steps - 1), 0)
    tile = pl.BlockSpec((TILE, width), rows)
    broad = pl.BlockSpec((TILE, parts * width), rows)
    tokens = jax.ShapeDtypeStruct((length, width), BF16)
    return pl.pallas_call(
        functools.partial(feed_back_kernel, width, steps),
        grid=(steps + 1,),
        in_specs=[tile, tile, tile, broad, broad] + weight_specs(width, parts, (0, 1, 2, 3))
        + [pl.BlockSpec(memory_space=pl.ANY)] * len(deps),
        out_specs=[
            tile, tile, tile,
            pl.BlockSpec((16, TILE), lambda g: (0, jnp.minimum(g, steps - 1))),
            pl.BlockSpec((width, width), lambda g: (0, 0)),
        ],
        out_shape=[
            tokens,
            jax.ShapeDtypeStruct((length, width), F32),
            tokens,
            jax.ShapeDtypeStruct((16, length), F32),
            jax.ShapeDtypeStruct((width, width), BF16),
        ],
        scratch_shapes=[pltpu.VMEM((length, width), BF16)] * 2,
        compiler_params=pltpu.CompilerParams(vmem_limit_bytes=58 * 1024 * 1024),
        cost_estimate=SMALL,
        name="feed_back",
    )(attended, middle, upstream, act, back, weights, weights, weights, gain, *deps)


def last_kernel(start_ref, middle_ref, gain_ref, weight_ref, *rest):
    grads_refs, out_ref = rest[:1], rest[-1]
    start = start_ref[...]
    gain = gain_ref[...]
    root = lax.rsqrt(jnp.mean(start * start, axis=1, keepdims=True) + 1e-06)
    scaled = start * root
    low = 0
    back = 0.0
    for grads_ref in grads_refs:
        high = low + grads_ref.shape[1]
        back = back + dot(grads_ref[...], weight_ref[:, low:high], NT)
        low = high
    slant = jnp.mean(back * scaled * gain, axis=1, keepdims=True)
    out_ref[...] = middle_ref[...] + root * (gain * back - scaled * slant)


def last(start, middle, gain, weights, grads, *deps):
    length, width = start.shape
    tile = pl.BlockSpec((TILE, width), lambda g: (g, 0))
    total = sum(item.shape[1] for item in grads)
    return pl.pallas_call(
        last_kernel,
        grid=(length // TILE,),
        in_specs=[
            tile, tile, pl.BlockSpec((1, width), lambda g: (0, 0)),
            pl.BlockSpec((width, total), lambda g: (0, 0), pipeline_mode=pl.Buffered(1)),
        ]
        + [pl.BlockSpec((TILE, item.shape[1]), lambda g: (g, 0)) for item in grads]
        + [pl.BlockSpec(memory_space=pl.ANY)] * len(deps),
        out_specs=tile,
        out_shape=jax.ShapeDtypeStruct((length, width), F32),
        compiler_params=pltpu.CompilerParams(vmem_limit_bytes=24 * 1024 * 1024),
        cost_estimate=SMALL,
        name="last",
    )(start, middle, gain, weights, *grads, *deps)


def half_kernel(count, core_ref, *refs):
    out_ref = refs[-1]
    low = 0
    for array_ref in refs[:count]:
        high = low + array_ref.shape[-1]
        for place in range(array_ref.shape[0]):
            out_ref[0, place, :, low:high] = array_ref[place, 0, 0]
        low = high


def merge_kernel(count, core_ref, *refs):
    came_ref, out_ref = refs[count], refs[-1]
    low = 0
    for array_ref in refs[:count]:
        high = low + array_ref.shape[-1]
        for place in range(array_ref.shape[0]):
            out_ref[0, place, :, low:high] = (
                array_ref[place, 0, 0].astype(F32) + came_ref[0, place, :, low:high].astype(F32)
            ).astype(BF16)
        low = high


def core_part(kernel, core, arrays, owned, came, *deps):
    outer = arrays[0].shape[0] // owned // 8
    width = sum(array.shape[1] for array in arrays)
    block = pl.BlockSpec((1, outer, owned, width), lambda g, core: (g, 0, 0, 0))
    return pl.pallas_call(
        functools.partial(kernel, len(arrays)),
        grid_spec=pltpu.PrefetchScalarGridSpec(
            num_scalar_prefetch=1,
            grid=(4,),
            in_specs=[
                pl.BlockSpec((outer, 1, 1, owned, array.shape[1]), lambda g, core: (0, g, core[0], 0, 0)) for array in arrays
            ]
            + [block] * len(came) + [pl.BlockSpec(memory_space=pl.ANY)] * len(deps),
            out_specs=block,
        ),
        out_shape=jax.ShapeDtypeStruct((4, outer, owned, width), BF16),
        compiler_params=pltpu.CompilerParams(vmem_limit_bytes=20 * 1024 * 1024),
        cost_estimate=SMALL,
        name="core_part",
    )(core, *[array.reshape(outer, 4, 2, owned, array.shape[1]) for array in arrays], *came, *deps)


def gate_kernel(*refs):
    pass


def gate(array, *deps):
    return pl.pallas_call(
        gate_kernel,
        in_specs=[pl.BlockSpec(memory_space=pl.ANY)] * (1 + len(deps)),
        out_specs=pl.BlockSpec(memory_space=pl.ANY),
        out_shape=jax.ShapeDtypeStruct(array.shape, array.dtype),
        input_output_aliases={0: 0},
        cost_estimate=SMALL,
        name="gate",
    )(array, *deps)


def gather_sum_kernel(array_ref, *rest):
    out_ref = rest[-1]
    total = array_ref[0].astype(F32)
    for place in range(1, array_ref.shape[0]):
        total = total + array_ref[place].astype(F32)
    out_ref[...] = total.astype(out_ref.dtype)


def gather_sum(array, *deps):
    inner, outer, owned, width = array.shape
    return pl.pallas_call(
        gather_sum_kernel,
        grid=(outer,),
        in_specs=[pl.BlockSpec((inner, 1, owned, width), lambda g: (0, g, 0, 0))] + [pl.BlockSpec(memory_space=pl.ANY)] * len(deps),
        out_specs=pl.BlockSpec((1, owned, width), lambda g: (g, 0, 0)),
        out_shape=jax.ShapeDtypeStruct((outer, owned, width), BF16),
        compiler_params=pltpu.CompilerParams(vmem_limit_bytes=20 * 1024 * 1024),
        cost_estimate=SMALL,
        name="gather_sum",
    )(array, *deps)


def finish_kernel(width, level_ref, trio_ref, gain_ref, *out_refs):
    total = level_ref[0].astype(F32)
    for place in range(1, level_ref.shape[0]):
        total = total + level_ref[place].astype(F32)
    out_refs[0][...] = total[:, :width]
    for pair in range(width // LANES):
        for kind in range(3):
            low = width + (3 * pair + kind) * LANES
            out_refs[1 + kind][:, pair * LANES:(pair + 1) * LANES] = total[:, low:low + LANES]
    own = jnp.sum(trio_ref[...].astype(F32) * total[:, width:4 * width], axis=1, keepdims=True)
    out_refs[4][...] = jnp.broadcast_to(own / gain_ref[...].astype(F32), out_refs[4].shape)
    out_refs[5][...] = total[:, 4 * width:]


def finish(level, trio, gain):
    owned, width = trio.shape[0], trio.shape[1] // 3
    square = jax.ShapeDtypeStruct((owned, width), F32)
    return pl.pallas_call(
        functools.partial(finish_kernel, width),
        out_shape=[square] * 4 + [
            jax.ShapeDtypeStruct((owned, LANES), F32),
            jax.ShapeDtypeStruct((owned, level.shape[2] - 4 * width), F32),
        ],
        compiler_params=pltpu.CompilerParams(vmem_limit_bytes=20 * 1024 * 1024),
        cost_estimate=SMALL,
        name="finish",
    )(level, trio, gain)


def weave_kernel(core_ref, own_ref, came_ref, out_ref):
    core = core_ref[0]
    for place in range(own_ref.shape[0]):
        out_ref[0, place, core] = own_ref[place, 0]
        out_ref[0, place, 1 - core] = came_ref[place, 0]


def weave(core, own, came, width):
    inner, outer, owned = own.shape[:3]
    block = pl.BlockSpec((inner, 1, owned, width), lambda g, core: (0, g, 0, 0))
    return pl.pallas_call(
        weave_kernel,
        grid_spec=pltpu.PrefetchScalarGridSpec(
            num_scalar_prefetch=1,
            grid=(outer,),
            in_specs=[block, block],
            out_specs=pl.BlockSpec((1, inner, 2, owned, width), lambda g, core: (g, 0, 0, 0, 0)),
        ),
        out_shape=jax.ShapeDtypeStruct((outer, inner, 2, owned, width), BF16),
        compiler_params=pltpu.CompilerParams(vmem_limit_bytes=20 * 1024 * 1024),
        cost_estimate=SMALL,
        name="weave",
    )(core, own, came)


def turn(array, shift):
    return lax.dynamic_slice_in_dim(jnp.concatenate([array, array], axis=0), shift, array.shape[0], axis=0)


def long_start(segments):
    names = jnp.arange(8, dtype=jnp.int32)
    counts = jnp.sum((segments[None, :] == names[:, None]).astype(jnp.int32), axis=1)
    return jnp.sum((segments < jnp.argmax(counts).astype(jnp.int32)).astype(jnp.int32))


def member_groups(members, low, high):
    apart = 1 << low
    span = 1 << high
    return [
        [base + apart * place for place in range(span // apart)]
        for base in range(members)
        if (base & (span - 1) & ~(apart - 1)) == 0
    ]


def swap_cores(members, array):
    return lax.ppermute(array, "dp", [(place, place ^ 1) for place in range(members)])


def across_plane(members, array):
    return lax.all_to_all(array, "dp", 0, 0, axis_index_groups=member_groups(members, 1, 3))


def along_line(members, array):
    return lax.all_to_all(
        array, "dp", 0, 0, axis_index_groups=member_groups(members, 3, members.bit_length() - 1)
    )


def spread_line(members, array):
    outer = members // 8
    return lax.all_to_all(
        jnp.broadcast_to(array[None], (outer,) + array.shape), "dp", 0, 0,
        axis_index_groups=member_groups(members, 3, members.bit_length() - 1),
    )


def spread_plane(members, array):
    return across_plane(members, jnp.broadcast_to(array[None], (4,) + array.shape))


def per_device(
    members,
    tokens,
    image_features,
    segment_ids,
    box_left,
    box_top,
    cotangent,
    query_weight,
    key_weight,
    value_weight,
    output_weight,
    inner_weight,
    outer_weight,
    attention_gain,
    feed_gain,
    bias_tables,
):
    length, width = tokens.shape[1:]
    owned = query_weight.shape[0]
    parts = inner_weight.shape[1] // width
    spots = bias_tables.shape[0]

    small = jnp.concatenate(
        [
            attention_gain[:, None],
            feed_gain[:, None],
            jnp.pad(bias_tables, (0, 2 * owned - spots)).reshape(owned, 2),
            jnp.zeros((owned, LANES - 4), BF16),
        ],
        axis=1,
    )
    pairs = width // LANES
    trio = jnp.concatenate([query_weight, key_weight, value_weight], axis=1)
    trio = trio.reshape(owned, 3, pairs, LANES).transpose(0, 2, 1, 3).reshape(owned, 3 * width)
    core = (lax.axis_index("dp") & 1).reshape(1)
    inner_own = inner_weight.reshape(owned, width, parts).transpose(0, 2, 1).reshape(owned, parts * width)
    second = lax.all_gather(
        jnp.concatenate([inner_own, outer_weight.reshape(owned, parts * width), output_weight], axis=1),
        "dp", axis=0, tiled=True,
    )
    shift = long_start(segment_ids[0])
    segments, left, top = (turn(item[0], shift) for item in (segment_ids, box_left, box_top))
    start = turn(tokens[0], shift).astype(F32) + turn(image_features[0], shift).astype(F32)
    upstream = turn(cotangent[0], shift)
    root = lax.rsqrt(jnp.mean(start * start, axis=1, keepdims=True) + 1e-06)
    level = spread_line(members, jnp.concatenate([trio, small], axis=1))
    part = spread_plane(members, gate(level[:, :, 3 * width:], start))
    level = spread_plane(members, level[:, :, :3 * width])
    little = weave(core, part, swap_cores(members, part), LANES).reshape(width, LANES)
    gain_one = little[:, 0].astype(F32)[None]
    gain_two = little[:, 1].astype(F32)[None]
    bands = rows_of(little[:, 2:4].reshape(-1, 2 * owned)[:, :spots].reshape(3 * BUCKETS, HEADS))
    normed = (start * root * gain_one).astype(BF16)
    columns = [segments[:, None], left[:, None], top[:, None]]
    level = gate(level, upstream, normed, gain_two, bands, *columns)
    project = weave(core, level, swap_cores(members, level), 3 * width).reshape(width, 3 * width)
    scale = jnp.where(jnp.arange(3 * width) % (3 * LANES) < LANES, 0.125, 1.0)[None]
    packed = (dot(normed, project) * scale).astype(BF16)
    attended, probs, inverse = attend(packed, bands, segments, left, top, columns)

    kept = parts // 2
    middle, act, inner_back, early, late = feed(kept, attended, start, upstream, second, gain_two)
    early_sum = lax.psum_scatter(early, "dp", scatter_dimension=0, tiled=True)
    sent = core_part(half_kernel, 1 - core, [late], owned, [])
    late_one = core_part(merge_kernel, core, [late], owned, [swap_cores(members, sent)])
    late_two = across_plane(members, late_one)

    layer, grad_middle, grad_attended, delta, output_grad = feed_back(
        attended, middle, upstream, act, inner_back, second, gain_two, late_one
    )
    late_two = gather_sum(late_two, delta)
    late_last = jnp.sum(along_line(members, late_two).astype(F32), axis=0)

    grads, weights, bands_grad = attend_back(
        0, pairs, packed, grad_attended, probs, inverse, delta, left, top, columns, normed, bucket_marks(), late_two
    )
    tables_grad = bands_grad[:, :3, :BUCKETS].transpose(1, 2, 0).reshape(-1)
    room = -(-tables_grad.size // owned // LANES) * LANES
    tables_grad = jnp.pad(tables_grad, (0, owned * room - tables_grad.size)).astype(BF16).reshape(1, owned, room)
    tables_grad = jnp.broadcast_to(tables_grad, (members, owned, room)).reshape(width, room)
    group = [output_grad, weights, tables_grad]
    sent = core_part(half_kernel, 1 - core, group, owned, [], late_last)
    trio_one = core_part(merge_kernel, core, group, owned, [swap_cores(members, sent)])
    trio_two = across_plane(members, trio_one)

    input_gradient = turn(last(start, grad_middle, gain_one, project, [grads], trio_one), length - shift)[None]
    layer = turn(gate(layer, trio_one), length - shift)[None]

    trio_two = gather_sum(trio_two, input_gradient, layer)
    outer_sum = early_sum[:, :parts * width].astype(F32).reshape(outer_weight.shape)
    inner_sum = jnp.concatenate([early_sum[:, parts * width:].astype(F32), late_last], axis=1)
    inner_sum = inner_sum.reshape(owned, parts, width).transpose(0, 2, 1).reshape(owned, parts * width)
    feed_gain_grad = jnp.sum(inner_weight.astype(F32) * inner_sum, axis=1) / feed_gain.astype(F32)
    output_sum, query_sum, key_sum, value_sum, gain_grad, tables_last = finish(
        gate(along_line(members, trio_two), inner_sum, outer_sum), trio, attention_gain[:, None]
    )
    tables_last = lax.dynamic_slice_in_dim(tables_last.reshape(-1), lax.axis_index("dp") * spots, spots)
    return (
        layer,
        input_gradient,
        query_sum,
        key_sum,
        value_sum,
        output_sum,
        inner_sum,
        outer_sum,
        gain_grad[:, 0],
        feed_gain_grad,
        tables_last,
    )


def solution(mesh):
    rows = P("dp", None)
    cubes = P("dp", None, None)
    line = P("dp")
    return jax.shard_map(
        functools.partial(per_device, mesh.shape["dp"]),
        mesh=mesh,
        in_specs=(cubes, cubes, rows, rows, rows, cubes) + (rows,) * 6 + (line,) * 3,
        out_specs=(cubes, cubes) + (rows,) * 6 + (line,) * 3,
        check_vma=False,
    )
```

profile of v0, /device:TPU:0, one launch (start us, length us, event | category | flops | bytes accessed | tf_op | source)
XLA Modules:
  0.0 317.0 jit_solution(12076423365162580382)
XLA Ops:
  13.5 6.3 %all-to-all-start = ((bf16[4,24,2432]{2,1,0:T(8,128)(2,1)}), bf16[4,24,2432]{2,1,0:T(8,128)(2,1)S(1)}, u32[]{:S(2)}, u32[]{:S(2)}) async-start(bf16[4,24,2432]{2,1,0:T(8,128)(2,1)} %broadcast_in_dim.75), calls=%async_computation | async-start | bytes 933888 | tf_op jit(solution)/shard_map/all_to_all | solution.py:739
  23.8 5.2 %multiply_reduce_fusion = (f32[1024]{0:T(1024)S(1)}, f32[1024,768]{1,0:T(8,128)}) fusion(s32[]{:T(128)S(6)} %select_n.38, bf16[1024,768]{1,0:T(8,128)(2,1)S(1)} %bitcast.63, bf16[1024,768]{1,0:T(8,128)(2,1)} %bitcast.64), kind=kLoop, calls=%fused_computation.14 | loop fusion | flops 8649728 | bytes 6295556 | tf_op jit(solution)/shard_map/reduce_sum | solution.py:794
  29.1 9.4 %all-to-all-done = bf16[4,24,2432]{2,1,0:T(8,128)(2,1)S(1)} async-done(((bf16[4,24,2432]{2,1,0:T(8,128)(2,1)}), bf16[4,24,2432]{2,1,0:T(8,128)(2,1)S(1)}, u32[]{:S(2)}, u32[]{:S(2)}) %all-to-all-start) | async-done | bytes 466976 | tf_op jit(solution)/shard_map/all_to_all | solution.py:739
  40.4 3.7 %all-to-all-start.1 = ((bf16[4,4,24,128]{3,2,1,0:T(8,128)(2,1)}), bf16[4,4,24,128]{3,2,1,0:T(8,128)(2,1)S(1)}, u32[]{:S(2)}, u32[]{:S(2)}) async-start(bf16[4,4,24,128]{3,2,1,0:T(8,128)(2,1)} %broadcast_in_dim.76), calls=%async_computation.1 | async-start | bytes 196608 | tf_op jit(solution)/shard_map/all_to_all | solution.py:728
  46.3 2.9 all-to-all-done.1.own_ref
  50.5 4.4 %all-to-all-start.2 = ((bf16[4,4,24,2304]{3,2,1,0:T(8,128)(2,1)}), bf16[4,4,24,2304]{3,2,1,0:T(8,128)(2,1)}, u32[]{:S(2)}, u32[]{:S(2)}) async-start(bf16[4,4,24,2304]{3,2,1,0:T(8,128)(2,1)} %broadcast_in_dim.77), calls=%async_computation.2 | async-start | bytes 3538944 | tf_op jit(solution)/shard_map/all_to_all | solution.py:728
  57.2 4.4 %fusion.4.refs_1_.up_ref = bf16[1024,768]{1,0:T(8,128)(2,1)} fusion(s32[]{:T(128)S(6)} %select_n.38, bf16[1024,768]{1,0:T(8,128)(2,1)} %bitcast.65), kind=kLoop, calls=%fused_computation.18 | loop fusion | flops 3145728 | bytes 3145732 | tf_op jit(solution)/shard_map/concatenate | solution.py:704
  69.1 7.9 %all-to-all-done.2.refs_0_ = bf16[4,4,24,2304]{3,2,1,0:T(8,128)(2,1)} async-done(((bf16[4,4,24,2304]{3,2,1,0:T(8,128)(2,1)}), bf16[4,4,24,2304]{3,2,1,0:T(8,128)(2,1)}, u32[]{:S(2)}, u32[]{:S(2)}) %all-to-all-start.2) | async-done | bytes 1769504 | tf_op jit(solution)/shard_map/all_to_all | solution.py:728
  77.0 4.8 %collective-permute-done.1.came_ref = bf16[4,4,24,2304]{3,2,1,0:T(8,128)(2,1)S(1)} collective-permute-done((bf16[4,4,24,2304]{3,2,1,0:T(8,128)(2,1)}, bf16[4,4,24,2304]{3,2,1,0:T(8,128)(2,1)S(1)}, u32[]{:S(2)}, u32[]{:S(2)}) %collective-permute-start.1) | collective-permute-done | bytes 1769504 | tf_op jit(solution)/shard_map/ppermute | solution.py:724
  84.2 5.5 %multiply_convert_fusion.qkv_ref = bf16[1024,2304]{1,0:T(8,128)(2,1)} fusion(bf16[1024,768]{1,0:T(8,128)(2,1)S(1)} %copy-done.17, bf16[768,2304]{1,0:T(8,128)(2,1)S(1)} %bitcast.50, f32[2304]{0:T(1024)S(1)} %fusion.14), kind=kOutput, calls=%fused_computation | convolution fusion | flops 3628597248 | bytes 9839616 | tf_op jit(solution)/shard_map/dot_general | solution.py:34
  89.7 24.6 %attend.1 = (bf16[1024,768]{1,0:T(8,128)(2,1)}, bf16[12,1024,512]{2,1,0:T(8,128)(2,1)}, f32[12,1,1024]{2,1,0:T(1,128)}) custom-call(bf16[1024,2304]{1,0:T(8,128)(2,1)} %multiply_convert_fusion.qkv_ref, f32[12,8,512]{2,1,0:T(8,128)} %copy.68.refs_4_.band_ref, s32[1024,1]{1,0:T(8,128)} %copy.69.refs_5_.seg_ref, s32[1,1024]{1,0:T(1,128)} %bitcast.79, ...), custom_call_target="tpu_custom_call" | custom-call | flops 100000000 | bytes 100000 | tf_op jit(solution)/shard_map/attend/pallas_call | solution.py:151
  114.3 36.4 %feed.1 = (f32[1024,768]{1,0:T(8,128)}, bf16[1024,3072]{1,0:T(8,128)(2,1)}, bf16[1024,3072]{1,0:T(8,128)(2,1)}, bf16[768,4608]{1,0:T(8,128)(2,1)}, bf16[768,1536]{1,0:T(8,128)(2,1)}) custom-call(bf16[1024,768]{1,0:T(8,128)(2,1)} %get-tuple-element.35.att_ref, f32[1024,768]{1,0:T(8,128)} %get-tuple-element.80.refs_1_.start_ref, ...), custom_call_target="tpu_custom_call" | custom-call | flops 100000000 | bytes 100000 | tf_op jit(solution)/shard_map/feed/pallas_call | solution.py:434
  152.8 2.7 collective-permute-done.2.refs_1_
  157.3 3.9 %all-to-all-start.3 = ((bf16[4,4,24,1536]{3,2,1,0:T(8,128)(2,1)}), bf16[4,4,24,1536]{3,2,1,0:T(8,128)(2,1)S(1)}, u32[]{:S(2)}, u32[]{:S(2)}) async-start(bf16[4,4,24,1536]{3,2,1,0:T(8,128)(2,1)} %core_part.5.rest_0_), calls=%async_computation.3 | async-start | bytes 2359296 | tf_op jit(solution)/shard_map/all_to_all | solution.py:728
  161.2 23.4 %feed_back.1 = (bf16[1024,768]{1,0:T(8,128)(2,1)}, f32[1024,768]{1,0:T(8,128)}, bf16[1024,768]{1,0:T(8,128)(2,1)}, f32[16,1024]{1,0:T(8,128)}, bf16[768,768]{1,0:T(8,128)(2,1)}) custom-call(bf16[1024,768]{1,0:T(8,128)(2,1)} %get-tuple-element.35.att_ref, f32[1024,768]{1,0:T(8,128)} %get-tuple-element.36.middle_ref, bf16[1024,768]{1,0:T(8,128)(2,1)} %fusion.4.refs_1_.up_ref, ...), custom_call_target="tpu_custom_call" | custom-call | flops 100000000 | bytes 100000 | tf_op jit(solution)/shard_map/feed_back/pallas_call | solution.py:506
  187.0 4.9 %all-to-all-start.4 = ((bf16[4,24,1536]{2,1,0:T(8,128)(2,1)}), bf16[4,24,1536]{2,1,0:T(8,128)(2,1)S(1)}, u32[]{:S(2)}, u32[]{:S(2)}) async-start(bf16[4,24,1536]{2,1,0:T(8,128)(2,1)} %gather_sum.2.rest_0_), calls=%async_computation.4 | async-start | bytes 589824 | tf_op jit(solution)/shard_map/all_to_all | solution.py:732
  191.8 40.7 %attend_back.1 = (bf16[1024,2304]{1,0:T(8,128)(2,1)}, bf16[768,2304]{1,0:T(8,128)(2,1)}, f32[12,8,128]{2,1,0:T(8,128)}) custom-call(bf16[1024,2304]{1,0:T(8,128)(2,1)} %multiply_convert_fusion.qkv_ref, bf16[1024,768]{1,0:T(8,128)(2,1)} %get-tuple-element.42.g_ref, bf16[12,1024,512]{2,1,0:T(8,128)(2,1)} %get-tuple-element.43.probs_ref, ...), custom_call_target="tpu_custom_call" | custom-call | flops 100000000 | bytes 100000 | tf_op jit(solution)/shard_map/attend_back/pallas_call | solution.py:316
  236.7 4.7 %collective-permute-done.3.refs_3_ = bf16[4,4,24,3200]{3,2,1,0:T(8,128)(2,1)S(1)} collective-permute-done((bf16[4,4,24,3200]{3,2,1,0:T(8,128)(2,1)S(1)}, bf16[4,4,24,3200]{3,2,1,0:T(8,128)(2,1)S(1)}, u32[]{:S(2)}, u32[]{:S(2)}) %collective-permute-start.3) | collective-permute-done | bytes 2457632 | tf_op jit(solution)/shard_map/ppermute | solution.py:724
  243.8 4.9 %all-to-all-start.5 = ((bf16[4,4,24,3200]{3,2,1,0:T(8,128)(2,1)}), bf16[4,4,24,3200]{3,2,1,0:T(8,128)(2,1)}, u32[]{:S(2)}, u32[]{:S(2)}) async-start(bf16[4,4,24,3200]{3,2,1,0:T(8,128)(2,1)} %core_part.7.refs_1_.rest_1_), calls=%async_computation.5 | async-start | bytes 4915200 | tf_op jit(solution)/shard_map/all_to_all | solution.py:728
  256.9 5.3 %last.1 = f32[1024,768]{1,0:T(8,128)S(1)} custom-call(f32[1024,768]{1,0:T(8,128)S(1)} %copy-done.1, f32[1024,768]{1,0:T(8,128)S(1)} %copy-done.12, f32[1,768]{1,0:T(1,128)S(1)} %convert_bitcast_fusion.gain_ref, bf16[768,2304]{1,0:T(8,128)(2,1)S(1)} %bitcast.51, bf16[1024,2304]{1,0:T(8,128)(2,1)S(1)} %copy-done.11, ...), custom_call_target="tpu_custom_call" | custom-call | flops 100000000 | bytes 100000 | tf_op jit(solution)/shard_map/last/pallas_call | solution.py:550
  262.2 3.8 %fusion.3.rest_1_ = bf16[1,1024,768]{2,1,0:T(8,128)(2,1)} fusion(s32[]{:T(128)S(6)} %select_n.41, bf16[1024,768]{1,0:T(8,128)(2,1)S(1)} %copy-done.20), kind=kLoop, calls=%fused_computation.17 | loop fusion | flops 3145728 | bytes 3145732 | tf_op jit(solution)/shard_map/broadcast_in_dim | solution.py:836
  267.6 12.3 %all-to-all-done.5.array_ref = bf16[4,4,24,3200]{3,2,1,0:T(8,128)(2,1)} async-done(((bf16[4,4,24,3200]{3,2,1,0:T(8,128)(2,1)}), bf16[4,4,24,3200]{3,2,1,0:T(8,128)(2,1)}, u32[]{:S(2)}, u32[]{:S(2)}) %all-to-all-start.5) | async-done | bytes 2457632 | tf_op jit(solution)/shard_map/all_to_all | solution.py:728
  284.7 5.1 %all-to-all-start.6 = ((bf16[4,24,3200]{2,1,0:T(8,128)(2,1)}), bf16[4,24,3200]{2,1,0:T(8,128)(2,1)S(1)}, u32[]{:S(2)}, u32[]{:S(2)}) async-start(bf16[4,24,3200]{2,1,0:T(8,128)(2,1)} %copy-done.13), calls=%async_computation.6 | async-start | bytes 1228800 | tf_op jit(solution)/shard_map/all_to_all | solution.py:732
  295.5 10.4 %all-to-all-done.6.refs_0_ = bf16[4,24,3200]{2,1,0:T(8,128)(2,1)S(1)} async-done(((bf16[4,24,3200]{2,1,0:T(8,128)(2,1)}), bf16[4,24,3200]{2,1,0:T(8,128)(2,1)S(1)}, u32[]{:S(2)}, u32[]{:S(2)}) %all-to-all-start.6) | async-done | bytes 614432 | tf_op jit(solution)/shard_map/all_to_all | solution.py:732
  (159 shorter events, 61.0 us)
Async XLA Ops:
  7.2 12.6 %copy-start.27 = (s32[1,1024]{1,0:T(1,128)S(1)}, s32[1,1024]{1,0:T(1,128)}, u32[]{:S(2)}) copy-start(s32[1,1024]{1,0:T(1,128)} %param.19) | copy-start | bytes 12292
  7.3 16.5 %copy-start.21 = (bf16[1,1024,768]{2,1,0:T(8,128)(2,1)S(1)}, bf16[1,1024,768]{2,1,0:T(8,128)(2,1)}, u32[]{:S(2)}) copy-start(bf16[1,1024,768]{2,1,0:T(8,128)(2,1)} %param.18) | copy-start | bytes 4718596
  7.3 107.1 %all-gather.2.cloned.1.call-start = ((), (), s32[]{:S(2)}) async-start(), calls=%async_computation.8 | async-start | bytes 10948608 | tf_op jit(solution)/shard_map/all_gather | solution.py:786
  12.1 17.0 %copy-start.15 = (bf16[24,1]{1,0:T(8,128)(2,1)}, bf16[24,1]{1,0:T(8,128)(2,1)S(1)}, u32[]{:S(2)}) copy-start(bf16[24,1]{1,0:T(8,128)(2,1)S(1)} %copy.64.gain_ref) | copy-start | bytes 148
  13.5 24.9 %all-to-all-start = ((bf16[4,24,2432]{2,1,0:T(8,128)(2,1)}), bf16[4,24,2432]{2,1,0:T(8,128)(2,1)S(1)}, u32[]{:S(2)}, u32[]{:S(2)}) async-start(bf16[4,24,2432]{2,1,0:T(8,128)(2,1)} %broadcast_in_dim.75), calls=%async_computation | async-start | bytes 933888 | tf_op jit(solution)/shard_map/all_to_all | solution.py:739
  29.0 15.1 %copy-start.31 = (s32[1,1024]{1,0:T(1,128)S(1)}, s32[1,1024]{1,0:T(1,128)}, u32[]{:S(2)}) copy-start(s32[1,1024]{1,0:T(1,128)} %param.21) | copy-start | bytes 12292
  29.1 15.1 %copy-start.32 = (s32[1,1024]{1,0:T(1,128)S(1)}, s32[1,1024]{1,0:T(1,128)}, u32[]{:S(2)}) copy-start(s32[1,1024]{1,0:T(1,128)} %param.20) | copy-start | bytes 12292
  40.4 8.8 %all-to-all-start.1 = ((bf16[4,4,24,128]{3,2,1,0:T(8,128)(2,1)}), bf16[4,4,24,128]{3,2,1,0:T(8,128)(2,1)S(1)}, u32[]{:S(2)}, u32[]{:S(2)}) async-start(bf16[4,4,24,128]{3,2,1,0:T(8,128)(2,1)} %broadcast_in_dim.76), calls=%async_computation.1 | async-start | bytes 196608 | tf_op jit(solution)/shard_map/all_to_all | solution.py:728
  50.5 26.5 %all-to-all-start.2 = ((bf16[4,4,24,2304]{3,2,1,0:T(8,128)(2,1)}), bf16[4,4,24,2304]{3,2,1,0:T(8,128)(2,1)}, u32[]{:S(2)}, u32[]{:S(2)}) async-start(bf16[4,4,24,2304]{3,2,1,0:T(8,128)(2,1)} %broadcast_in_dim.77), calls=%async_computation.2 | async-start | bytes 3538944 | tf_op jit(solution)/shard_map/all_to_all | solution.py:728
  54.9 234.9 %reduce-scatter.2.cloned.1.call-start = ((), (), s32[]{:S(2)}) async-start(), calls=%async_computation.9 | async-start | bytes 7299072 | tf_op jit(solution)/shard_map/reduce_scatter | solution.py:812
  55.6 11.4 %copy-start.28 = (s32[1024]{0:T(1024)}, s32[1024]{0:T(1024)S(1)}, u32[]{:S(2)}) copy-start(s32[1024]{0:T(1024)S(1)} %fusion.17) | copy-start | bytes 12292
  56.6 10.3 %copy-start = (f32[1024,768]{1,0:T(8,128)S(1)}, f32[1024,768]{1,0:T(8,128)}, u32[]{:S(2)}) copy-start(f32[1024,768]{1,0:T(8,128)} %get-tuple-element.80.refs_1_.start_ref) | copy-start | bytes 9437188
  57.2 4.4 %collective-permute-start = (bf16[4,4,24,128]{3,2,1,0:T(8,128)(2,1)S(1)}, bf16[4,4,24,128]{3,2,1,0:T(8,128)(2,1)S(1)}, u32[]{:S(2)}, u32[]{:S(2)}) collective-permute-start(bf16[4,4,24,128]{3,2,1,0:T(8,128)(2,1)S(1)} %all-to-all-done.1.own_ref), channel_id=1, source_target_pairs={{0,1},{1,0},{2,3},{3,2},{4,5},{5,4},{6,7},{7,6},{8,9},{9,8},{10,11... | collective-permute-start | bytes 294920 | tf_op jit(solution)/shard_map/ppermute | solution.py:724
  77.0 4.8 %collective-permute-start.1 = (bf16[4,4,24,2304]{3,2,1,0:T(8,128)(2,1)}, bf16[4,4,24,2304]{3,2,1,0:T(8,128)(2,1)S(1)}, u32[]{:S(2)}, u32[]{:S(2)}) collective-permute-start(bf16[4,4,24,2304]{3,2,1,0:T(8,128)(2,1)} %gate.5.own_ref), channel_id=1, source_target_pairs={{0,1},{1,0},{2,3},{3,2},{4,5},{5,4},{6,7},{7,6},{8,9},{9,8},{10,11... | collective-permute-start | bytes 5308424 | tf_op jit(solution)/shard_map/ppermute | solution.py:724
  77.0 7.2 %copy-start.17 = (bf16[1024,768]{1,0:T(8,128)(2,1)S(1)}, bf16[1024,768]{1,0:T(8,128)(2,1)}, u32[]{:S(2)}) copy-start(bf16[1024,768]{1,0:T(8,128)(2,1)} %multiply_convert_fusion.1.refs_2_.normed_ref) | copy-start | bytes 4718596
  152.7 2.9 collective-permute-start.2
  157.3 27.3 %all-to-all-start.3 = ((bf16[4,4,24,1536]{3,2,1,0:T(8,128)(2,1)}), bf16[4,4,24,1536]{3,2,1,0:T(8,128)(2,1)S(1)}, u32[]{:S(2)}, u32[]{:S(2)}) async-start(bf16[4,4,24,1536]{3,2,1,0:T(8,128)(2,1)} %core_part.5.rest_0_), calls=%async_computation.3 | async-start | bytes 2359296 | tf_op jit(solution)/shard_map/all_to_all | solution.py:728
  187.0 46.7 %all-to-all-start.4 = ((bf16[4,24,1536]{2,1,0:T(8,128)(2,1)}), bf16[4,24,1536]{2,1,0:T(8,128)(2,1)S(1)}, u32[]{:S(2)}, u32[]{:S(2)}) async-start(bf16[4,24,1536]{2,1,0:T(8,128)(2,1)} %gather_sum.2.rest_0_), calls=%async_computation.4 | async-start | bytes 589824 | tf_op jit(solution)/shard_map/all_to_all | solution.py:732
  191.8 41.9 %copy-start.10 = (bf16[768,768]{1,0:T(8,128)(2,1)S(1)}, bf16[768,768]{1,0:T(8,128)(2,1)}, u32[]{:S(2)}) copy-start(bf16[768,768]{1,0:T(8,128)(2,1)} %get-tuple-element.41) | copy-start | bytes 3538948
  236.6 4.7 %collective-permute-start.3 = (bf16[4,4,24,3200]{3,2,1,0:T(8,128)(2,1)S(1)}, bf16[4,4,24,3200]{3,2,1,0:T(8,128)(2,1)S(1)}, u32[]{:S(2)}, u32[]{:S(2)}) collective-permute-start(bf16[4,4,24,3200]{3,2,1,0:T(8,128)(2,1)S(1)} %core_part.6), channel_id=1, source_target_pairs={{0,1},{1,0},{2,3},{3,2},{4,5},{5,4},{6,7},{7,6},{8,9},{9,8},{10,11... | collective-permute-start | bytes 7372808 | tf_op jit(solution)/shard_map/ppermute | solution.py:724
  243.8 36.1 %all-to-all-start.5 = ((bf16[4,4,24,3200]{3,2,1,0:T(8,128)(2,1)}), bf16[4,4,24,3200]{3,2,1,0:T(8,128)(2,1)}, u32[]{:S(2)}, u32[]{:S(2)}) async-start(bf16[4,4,24,3200]{3,2,1,0:T(8,128)(2,1)} %core_part.7.refs_1_.rest_1_), calls=%async_computation.5 | async-start | bytes 4915200 | tf_op jit(solution)/shard_map/all_to_all | solution.py:728
  267.5 16.3 %copy-start.5 = (f32[1,1024,768]{2,1,0:T(8,128)}, f32[1,1024,768]{2,1,0:T(8,128)S(1)}, u32[]{:S(2)}) copy-start(f32[1,1024,768]{2,1,0:T(8,128)S(1)} %fusion.1.rest_0_) | copy-start | bytes 9437188
  284.7 21.2 %all-to-all-start.6 = ((bf16[4,24,3200]{2,1,0:T(8,128)(2,1)}), bf16[4,24,3200]{2,1,0:T(8,128)(2,1)S(1)}, u32[]{:S(2)}, u32[]{:S(2)}) async-start(bf16[4,24,3200]{2,1,0:T(8,128)(2,1)} %copy-done.13), calls=%async_computation.6 | async-start | bytes 1228800 | tf_op jit(solution)/shard_map/all_to_all | solution.py:732
  293.4 13.4 %copy-start.16 = (bf16[24,1]{1,0:T(8,128)(2,1)S(1)}, bf16[24,1]{1,0:T(8,128)(2,1)}, u32[]{:S(2)}) copy-start(bf16[24,1]{1,0:T(8,128)(2,1)} %copy-done.15) | copy-start | bytes 148
  (26 other events, 92.4 us)
Sparse Core Ops, SparseCore 0:
  12.0 99.7 all-gather.1
  150.9 127.8 reduce-scatter.1
where the time goes:
time: 323 us; the launch traced here: 317 us
  Pallas kernels  143 us (44%)
  waiting for transfers between devices  55.1 us (17%)
  local copies, waits for them, and re-layouts  35.2 us (11%)
  starting transfers between devices  34 us (11%)
  other arithmetic  24.6 us (8%)
  between operations  18.5 us (6%)
  matrix products  6.88 us (2%)
    pallas_call x1, Pallas kernels, attend_back(): pl.pallas_call(functools.partial(attend_back_kernel, first), grid=(count,...  40.7 us
    pallas_call x1, Pallas kernels, feed(): pl.pallas_call(functools.partial(feed_kernel, width, steps, kept), grid=(...  36.4 us
    pallas_call x1, Pallas kernels, attend(): pl.pallas_call(attend_kernel, grid=(HEADS // 2,), in_specs=[pl.BlockSpec(...  24.6 us
    pallas_call x1, Pallas kernels, feed_back(): pl.pallas_call(functools.partial(feed_back_kernel, width, steps), grid=(s...  23.4 us
    all_to_all x4, waiting for transfers between devices, across_plane(): lax.all_to_all(array, 'dp', 0, 0, axis_index_groups=member_groups(members...  23.1 us
    unnamed x77, local copies, waits for them, and re-layouts  17 us
    all_to_all x4, starting transfers between devices, across_plane(): lax.all_to_all(array, 'dp', 0, 0, axis_index_groups=member_groups(members...  16.9 us
    ppermute x4, waiting for transfers between devices, swap_cores(): lax.ppermute(array, 'dp', [(place, place ^ 1) for place in range(members)])  12.2 us
  transfers between devices with their start and end apart: 13, of which 8 were waited for; matrix products, arithmetic and copies ran while one was open for 14% of the time, Pallas kernels for 33%

commit v1 on v0

--- a/solution.py
+++ b/solution.py
@@ -354,63 +354,84 @@
 ROOT = float(np.sqrt(2.0 / np.pi))
 
 
-def feed_kernel(width, steps, kept, att_ref, start_ref, up_ref, inner_ref, outer_ref, output_ref, gain_ref,
-                middle_ref, act_ref, back_ref, early_ref, late_ref, active, inner_back, normed, upstream):
+def feed_kernel(width, parts, att_ref, start_ref, up_ref, inner_ref, outer_ref, output_ref, gain_ref,
+                middle_ref, act_ref, back_ref, early_ref, late_ref, active, inner_back, normed):
     step = pl.program_id(0)
-    parts = inner_ref.shape[1] // width
-
-    @pl.when(step < steps)
-    def _():
-        size = att_ref.shape[0]
-        rows = pl.ds(pl.multiple_of(step * size, size), size)
-        up = up_ref[...]
-        upstream[rows, :] = up
-        middle = start_ref[...] + dot(att_ref[...], output_ref[...])
-        middle_ref[...] = middle
-        root = lax.rsqrt(jnp.mean(middle * middle, axis=1, keepdims=True) + 1e-06)
-        low = (middle * root * gain_ref[...]).astype(BF16)
-        normed[rows, :] = low
-
-        def products(part):
-            own = slice(part * width, (part + 1) * width)
-            return dot(low, inner_ref[:, own]), dot(up, outer_ref[:, own], NT)
-
-        def finish(part, point, reach):
-            own = slice(part * width, (part + 1) * width)
-            square = point * point
-            bend = jnp.tanh(ROOT * point * (1.0 + 0.044715 * square))
-            half = 0.5 + 0.5 * bend
-            act = (point * half).astype(BF16)
-            slope = half + (0.5 * ROOT) * point * (1.0 - bend * bend) * (1.0 + (3 * 0.044715) * square)
-            grads = (slope * reach).astype(BF16)
-            act_ref[:, own] = act
-            back_ref[:, own] = grads
-            active[rows, own] = act
-            inner_back[rows, own] = grads
-
-        held = products(0)
-        for part in range(1, parts):
-            following = products(part)
-            finish(part - 1, *held)
-            held = following
-        finish(parts - 1, *held)
-
-    @pl.when(jnp.logical_and(step >= steps, step < steps + parts))
-    def _():
-        own = pl.ds(pl.multiple_of((step - steps) * width, width), width)
-        early_ref[...] = dot(active[:, own], upstream[...], TN).astype(BF16)
-
-    def inner_grad():
-        own = pl.ds(pl.multiple_of((step - steps - parts) * width, width), width)
-        return dot(normed[...], inner_back[:, own], TN).astype(BF16)
-
-    @pl.when(jnp.logical_and(step >= steps + parts, step < steps + parts + kept))
-    def _():
-        early_ref[...] = inner_grad()
-
-    @pl.when(step >= steps + parts + kept)
-    def _():
-        late_ref[...] = inner_grad()
+    length = att_ref.shape[0]
+    halves = (slice(0, length // 2), slice(length // 2, length))
+
+    def products(rows):
+        return dot(normed[rows], inner_ref[...]), dot(up_ref[rows], outer_ref[...], NT)
+
+    def close(slot, rows, point, reach):
+        square = point * point
+        bend = jnp.tanh(ROOT * point * (1.0 + 0.044715 * square))
+        half = 0.5 + 0.5 * bend
+        act = (point * half).astype(BF16)
+        slope = half + (0.5 * ROOT) * point * (1.0 - bend * bend) * (1.0 + (3 * 0.044715) * square)
+        grads = (slope * reach).astype(BF16)
+        act_ref[rows] = act
+        back_ref[rows] = grads
+        active[slot, rows] = act
+        inner_back[slot, rows] = grads
+
+    def body(part):
+        goal = late_ref if part == parts else early_ref
+        if part == 0:
+            for rows in halves:
+                middle = start_ref[rows] + dot(att_ref[rows], output_ref[...])
+                middle_ref[rows] = middle
+                root = lax.rsqrt(jnp.mean(middle * middle, axis=1, keepdims=True) + 1e-06)
+                normed[rows] = (middle * root * gain_ref[...]).astype(BF16)
+        slot, before = part % 2, (part + 1) % 2
+        if part < parts:
+            held = products(halves[0])
+        if part > 0:
+            goal[:, :width] = dot(active[before], up_ref[...], TN).astype(BF16)
+        if part < parts:
+            close(slot, halves[0], *held)
+            held = products(halves[1])
+        if part > 0:
+            goal[:, width:] = dot(normed[...], inner_back[before], TN).astype(BF16)
+        if part < parts:
+            close(slot, halves[1], *held)
+
+    for part in range(parts + 1):
+        pl.when(step == part)(functools.partial(body, part))
+
+
+def feed(attended, start, upstream, weights, gain):
+    length, width = attended.shape
+    parts = weights.shape[1] // width // 2
+    once = pl.Buffered(1)
+    whole = pl.BlockSpec((length, width), lambda g: (0, 0), pipeline_mode=once)
+    column = pl.BlockSpec((length, width), lambda g: (0, jnp.minimum(g, parts - 1)))
+    tall = jax.ShapeDtypeStruct((length, parts * width), BF16)
+    return pl.pallas_call(
+        functools.partial(feed_kernel, width, parts),
+        grid=(parts + 1,),
+        in_specs=[
+            whole, whole, whole,
+            pl.BlockSpec((width, width), lambda g: (0, jnp.minimum(g, parts - 1))),
+            pl.BlockSpec((width, width), lambda g: (0, parts + jnp.minimum(g, parts - 1))),
+            pl.BlockSpec((width, width), lambda g: (0, 2 * parts), pipeline_mode=once),
+            pl.BlockSpec((1, width), lambda g: (0, 0)),
+        ],
+        out_specs=[
+            pl.BlockSpec((length, width), lambda g: (0, 0)), column, column,
+            pl.BlockSpec((width, 2 * width), lambda g: (0, jnp.clip(g - 1, 0, parts - 2))),
+            pl.BlockSpec((width, 2 * width), lambda g: (0, 0)),
+        ],
+        out_shape=[
+            jax.ShapeDtypeStruct((length, width), F32), tall, tall,
+            jax.ShapeDtypeStruct((width, 2 * (parts - 1) * width), BF16),
+            jax.ShapeDtypeStruct((width, 2 * width), BF16),
+        ],
+        scratch_shapes=[pltpu.VMEM((2, length, width), BF16)] * 2 + [pltpu.VMEM((length, width), BF16)],
+        compiler_params=pltpu.CompilerParams(vmem_limit_bytes=58 * 1024 * 1024),
+        cost_estimate=SMALL,
+        name="feed",
+    )(attended, start, upstream, weights, weights, weights, gain)
 
 
 def weight_specs(width, parts, places):
@@ -422,36 +443,6 @@
         pl.BlockSpec((1, width), lambda g: (0, 0)),
     ]
     return [specs[place] for place in places]
-
-
-def feed(kept, attended, start, upstream, weights, gain):
-    length, width = attended.shape
-    steps = length // TILE
-    parts = weights.shape[1] // width // 2
-    rows = lambda g: (jnp.minimum(g, steps - 1), 0)
-    tile = pl.BlockSpec((TILE, width), rows)
-    broad = pl.BlockSpec((TILE, parts * width), rows)
-    return pl.pallas_call(
-        functools.partial(feed_kernel, width, steps, kept),
-        grid=(steps + 2 * parts,),
-        in_specs=[tile, tile, tile] + weight_specs(width, parts, (0, 1, 2, 3)),
-        out_specs=[
-            tile, broad, broad,
-            pl.BlockSpec((width, width), lambda g: (0, jnp.clip(g - steps, 0, parts + kept - 1))),
-            pl.BlockSpec((width, width), lambda g: (0, jnp.maximum(g - steps - parts - kept, 0))),
-        ],
-        out_shape=[
-            jax.ShapeDtypeStruct((length, width), F32),
-            jax.ShapeDtypeStruct((length, parts * width), BF16),
-            jax.ShapeDtypeStruct((length, parts * width), BF16),
-            jax.ShapeDtypeStruct((width, (parts + kept) * width), BF16),
-            jax.ShapeDtypeStruct((width, (parts - kept) * width), BF16),
-        ],
-        scratch_shapes=[pltpu.VMEM((length, parts * width), BF16)] * 2 + [pltpu.VMEM((length, width), BF16)] * 2,
-        compiler_params=pltpu.CompilerParams(vmem_limit_bytes=58 * 1024 * 1024),
-        cost_estimate=SMALL,
-        name="feed",
-    )(attended, start, upstream, weights, weights, weights, gain)
 
 
 def feed_back_kernel(width, steps, att_ref, middle_ref, up_ref, act_ref, back_ref, inner_ref, outer_ref, output_ref, gain_ref,
@@ -793,22 +784,21 @@
     upstream = turn(cotangent[0], shift)
     root = lax.rsqrt(jnp.mean(start * start, axis=1, keepdims=True) + 1e-06)
     level = spread_line(members, jnp.concatenate([trio, small], axis=1))
-    part = spread_plane(members, gate(level[:, :, 3 * width:], start))
+    columns = [segments[:, None], left[:, None], top[:, None]]
+    part = spread_plane(members, gate(level[:, :, 3 * width:], start, upstream, *columns))
     level = spread_plane(members, level[:, :, :3 * width])
     little = weave(core, part, swap_cores(members, part), LANES).reshape(width, LANES)
     gain_one = little[:, 0].astype(F32)[None]
     gain_two = little[:, 1].astype(F32)[None]
     bands = rows_of(little[:, 2:4].reshape(-1, 2 * owned)[:, :spots].reshape(3 * BUCKETS, HEADS))
     normed = (start * root * gain_one).astype(BF16)
-    columns = [segments[:, None], left[:, None], top[:, None]]
     level = gate(level, upstream, normed, gain_two, bands, *columns)
     project = weave(core, level, swap_cores(members, level), 3 * width).reshape(width, 3 * width)
     scale = jnp.where(jnp.arange(3 * width) % (3 * LANES) < LANES, 0.125, 1.0)[None]
     packed = (dot(normed, project) * scale).astype(BF16)
     attended, probs, inverse = attend(packed, bands, segments, left, top, columns)
 
-    kept = parts // 2
-    middle, act, inner_back, early, late = feed(kept, attended, start, upstream, second, gain_two)
+    middle, act, inner_back, early, late = feed(attended, start, upstream, second, gain_two)
     early_sum = lax.psum_scatter(early, "dp", scatter_dimension=0, tiled=True)
     sent = core_part(half_kernel, 1 - core, [late], owned, [])
     late_one = core_part(merge_kernel, core, [late], owned, [swap_cores(members, sent)])
@@ -836,9 +826,9 @@
     layer = turn(gate(layer, trio_one), length - shift)[None]
 
     trio_two = gather_sum(trio_two, input_gradient, layer)
-    outer_sum = early_sum[:, :parts * width].astype(F32).reshape(outer_weight.shape)
-    inner_sum = jnp.concatenate([early_sum[:, parts * width:].astype(F32), late_last], axis=1)
-    inner_sum = inner_sum.reshape(owned, parts, width).transpose(0, 2, 1).reshape(owned, parts * width)
+    paired = jnp.concatenate([early_sum.astype(F32), late_last], axis=1).reshape(owned, parts, 2, width)
+    outer_sum = paired[:, :, 0].reshape(outer_weight.shape)
+    inner_sum = paired[:, :, 1].transpose(0, 2, 1).reshape(owned, parts * width)
     feed_gain_grad = jnp.sum(inner_weight.astype(F32) * inner_sum, axis=1) / feed_gain.astype(F32)
     output_sum, query_sum, key_sum, value_sum, gain_grad, tables_last = finish(
         gate(along_line(members, trio_two), inner_sum, outer_sum), trio, attention_gain[:, None]

time: 323 us -> 326 us (level); the launches traced: 317 us -> 325 us
  Pallas kernels: 143 us -> 152 us
    pallas_call x1, Pallas kernels: 36.4 us -> 46 us  [feed(): pl.pallas_call(functools.partial(feed_kernel, width, parts), grid=(parts...]
    all_to_all x4, waiting for transfers between devices: 23.1 us -> 28.8 us  [across_plane(): lax.all_to_all(array, 'dp', 0, 0, axis_index_groups=member_groups(members...]
    all_to_all x1, waiting for transfers between devices: 9.36 us -> 3.72 us  [spread_line(): lax.all_to_all(jnp.broadcast_to(array[None], (outer,) + array.shape), 'dp...]
    unnamed x77 -> x82, local copies, waits for them, and re-layouts: 17 us -> 19.4 us
  transfers between devices with their start and end apart: 13 -> 13, of which waited for: 8 -> 9; matrix products, arithmetic and copies ran while one was open for 14% -> 14% of each run, Pallas kernels for 33% -> 32%
where the time goes in v1:
time: 326 us; the launch traced here: 325 us
  Pallas kernels  152 us (47%)
  waiting for transfers between devices  54.2 us (17%)
  local copies, waits for them, and re-layouts  38.1 us (12%)
  starting transfers between devices  33.2 us (10%)
  other arithmetic  21.9 us (7%)
  between operations  18.4 us (6%)
  matrix products  6.9 us (2%)
    pallas_call x1, Pallas kernels, feed(): pl.pallas_call(functools.partial(feed_kernel, width, parts), grid=(parts...  46 us
    pallas_call x1, Pallas kernels, attend_back(): pl.pallas_call(functools.partial(attend_back_kernel, first), grid=(count,...  40.7 us
    all_to_all x4, waiting for transfers between devices, across_plane(): lax.all_to_all(array, 'dp', 0, 0, axis_index_groups=member_groups(members...  28.8 us
    pallas_call x1, Pallas kernels, attend(): pl.pallas_call(attend_kernel, grid=(HEADS // 2,), in_specs=[pl.BlockSpec(...  24.6 us
    pallas_call x1, Pallas kernels, feed_back(): pl.pallas_call(functools.partial(feed_back_kernel, width, steps), grid=(s...  23.4 us
    unnamed x82, local copies, waits for them, and re-layouts  19.4 us
    all_to_all x4, starting transfers between devices, across_plane(): lax.all_to_all(array, 'dp', 0, 0, axis_index_groups=member_groups(members...  16.6 us
    ppermute x4, waiting for transfers between devices, swap_cores(): lax.ppermute(array, 'dp', [(place, place ^ 1) for place in range(members)])  11.9 us
  transfers between devices with their start and end apart: 13, of which 9 were waited for; matrix products, arithmetic and copies ran while one was open for 14% of the time, Pallas kernels for 32%

profile of v1, /device:TPU:0, one launch (start us, length us, event | category | flops | bytes accessed | tf_op | source)
XLA Modules:
  0.0 325.2 jit_solution(5390288451167131332)
XLA Ops:
  13.6 6.3 %all-to-all-start = ((bf16[4,24,2432]{2,1,0:T(8,128)(2,1)}), bf16[4,24,2432]{2,1,0:T(8,128)(2,1)S(1)}, u32[]{:S(2)}, u32[]{:S(2)}) async-start(bf16[4,24,2432]{2,1,0:T(8,128)(2,1)} %broadcast_in_dim.75), calls=%async_computation | async-start | bytes 933888 | tf_op jit(solution)/shard_map/all_to_all | solution.py:730
  27.2 3.7 %fusion.4.refs_2_.refs_1_.up_ref = bf16[1024,768]{1,0:T(8,128)(2,1)} fusion(s32[]{:T(128)S(6)} %select_n.38, bf16[1024,768]{1,0:T(8,128)(2,1)S(1)} %bitcast.65), kind=kLoop, calls=%fused_computation.18 | loop fusion | flops 3145728 | bytes 3145732 | tf_op jit(solution)/shard_map/concatenate | solution.py:695
  30.9 3.9 %multiply_reduce_fusion = (f32[1024]{0:T(1024)S(1)}, f32[1024,768]{1,0:T(8,128)}) fusion(s32[]{:T(128)S(6)} %select_n.38, bf16[1024,768]{1,0:T(8,128)(2,1)S(1)} %bitcast.66, bf16[1024,768]{1,0:T(8,128)(2,1)S(1)} %bitcast.67), kind=kLoop, calls=%fused_computation.14 | loop fusion | flops 8649728 | bytes 6295556 | tf_op jit(solution)/shard_map/reduce_sum | solution.py:785
  34.8 3.7 %all-to-all-done = bf16[4,24,2432]{2,1,0:T(8,128)(2,1)S(1)} async-done(((bf16[4,24,2432]{2,1,0:T(8,128)(2,1)}), bf16[4,24,2432]{2,1,0:T(8,128)(2,1)S(1)}, u32[]{:S(2)}, u32[]{:S(2)}) %all-to-all-start) | async-done | bytes 466976 | tf_op jit(solution)/shard_map/all_to_all | solution.py:730
  40.5 3.7 %all-to-all-start.1 = ((bf16[4,4,24,128]{3,2,1,0:T(8,128)(2,1)}), bf16[4,4,24,128]{3,2,1,0:T(8,128)(2,1)S(1)}, u32[]{:S(2)}, u32[]{:S(2)}) async-start(bf16[4,4,24,128]{3,2,1,0:T(8,128)(2,1)} %broadcast_in_dim.79), calls=%async_computation.1 | async-start | bytes 196608 | tf_op jit(solution)/shard_map/all_to_all | solution.py:719
  44.3 5.0 %all-to-all-done.1.own_ref = bf16[4,4,24,128]{3,2,1,0:T(8,128)(2,1)S(1)} async-done(((bf16[4,4,24,128]{3,2,1,0:T(8,128)(2,1)}), bf16[4,4,24,128]{3,2,1,0:T(8,128)(2,1)S(1)}, u32[]{:S(2)}, u32[]{:S(2)}) %all-to-all-start.1) | async-done | bytes 98336 | tf_op jit(solution)/shard_map/all_to_all | solution.py:719
  50.6 4.6 %all-to-all-start.2 = ((bf16[4,4,24,2304]{3,2,1,0:T(8,128)(2,1)}), bf16[4,4,24,2304]{3,2,1,0:T(8,128)(2,1)}, u32[]{:S(2)}, u32[]{:S(2)}) async-start(bf16[4,4,24,2304]{3,2,1,0:T(8,128)(2,1)} %broadcast_in_dim.80), calls=%async_computation.2 | async-start | bytes 3538944 | tf_op jit(solution)/shard_map/all_to_all | solution.py:719
  66.2 11.5 %all-to-all-done.2.refs_0_ = bf16[4,4,24,2304]{3,2,1,0:T(8,128)(2,1)} async-done(((bf16[4,4,24,2304]{3,2,1,0:T(8,128)(2,1)}), bf16[4,4,24,2304]{3,2,1,0:T(8,128)(2,1)}, u32[]{:S(2)}, u32[]{:S(2)}) %all-to-all-start.2) | async-done | bytes 1769504 | tf_op jit(solution)/shard_map/all_to_all | solution.py:719
  77.7 3.9 %collective-permute-done.1.came_ref = bf16[4,4,24,2304]{3,2,1,0:T(8,128)(2,1)S(1)} collective-permute-done((bf16[4,4,24,2304]{3,2,1,0:T(8,128)(2,1)}, bf16[4,4,24,2304]{3,2,1,0:T(8,128)(2,1)S(1)}, u32[]{:S(2)}, u32[]{:S(2)}) %collective-permute-start.1) | collective-permute-done | bytes 1769504 | tf_op jit(solution)/shard_map/ppermute | solution.py:715
  84.0 5.5 %multiply_convert_fusion.qkv_ref = bf16[1024,2304]{1,0:T(8,128)(2,1)} fusion(bf16[1024,768]{1,0:T(8,128)(2,1)S(1)} %copy-done.19, bf16[768,2304]{1,0:T(8,128)(2,1)S(1)} %bitcast.52, f32[2304]{0:T(1024)S(1)} %fusion.14), kind=kOutput, calls=%fused_computation | convolution fusion | flops 3628597248 | bytes 9839616 | tf_op jit(solution)/shard_map/dot_general | solution.py:34
  89.5 24.6 %attend.1 = (bf16[1024,768]{1,0:T(8,128)(2,1)}, bf16[12,1024,512]{2,1,0:T(8,128)(2,1)}, f32[12,1,1024]{2,1,0:T(1,128)}) custom-call(bf16[1024,2304]{1,0:T(8,128)(2,1)} %multiply_convert_fusion.qkv_ref, f32[12,8,512]{2,1,0:T(8,128)} %copy.76.refs_4_.band_ref, s32[1024,1]{1,0:T(8,128)} %copy.71.refs_3_.refs_5_.seg_ref, s32[1,1024]{1,0:T(1,128)} %bitcast.81, ...), custom_call_target="tpu_custom_call" | custom-call | flops 100000000 | bytes 100000 | tf_op jit(solution)/shard_map/attend/pallas_call | solution.py:151
  114.1 46.0 %feed.1 = (f32[1024,768]{1,0:T(8,128)}, bf16[1024,3072]{1,0:T(8,128)(2,1)}, bf16[1024,3072]{1,0:T(8,128)(2,1)}, bf16[768,4608]{1,0:T(8,128)(2,1)}, bf16[768,1536]{1,0:T(8,128)(2,1)}) custom-call(bf16[1024,768]{1,0:T(8,128)(2,1)} %get-tuple-element.35.att_ref, f32[1024,768]{1,0:T(8,128)} %get-tuple-element.80.refs_1_.start_ref, ...), custom_call_target="tpu_custom_call" | custom-call | flops 100000000 | bytes 100000 | tf_op jit(solution)/shard_map/feed/pallas_call | solution.py:410
  162.3 2.7 collective-permute-done.2.refs_1_
  166.8 3.5 %all-to-all-start.3 = ((bf16[4,4,24,1536]{3,2,1,0:T(8,128)(2,1)}), bf16[4,4,24,1536]{3,2,1,0:T(8,128)(2,1)S(1)}, u32[]{:S(2)}, u32[]{:S(2)}) async-start(bf16[4,4,24,1536]{3,2,1,0:T(8,128)(2,1)} %core_part.5.rest_0_), calls=%async_computation.3 | async-start | bytes 2359296 | tf_op jit(solution)/shard_map/all_to_all | solution.py:719
  170.4 23.4 %feed_back.1 = (bf16[1024,768]{1,0:T(8,128)(2,1)}, f32[1024,768]{1,0:T(8,128)}, bf16[1024,768]{1,0:T(8,128)(2,1)}, f32[16,1024]{1,0:T(8,128)}, bf16[768,768]{1,0:T(8,128)(2,1)}) custom-call(bf16[1024,768]{1,0:T(8,128)(2,1)} %get-tuple-element.35.att_ref, f32[1024,768]{1,0:T(8,128)} %get-tuple-element.36.middle_ref, ...), custom_call_target="tpu_custom_call" | custom-call | flops 100000000 | bytes 100000 | tf_op jit(solution)/shard_map/feed_back/pallas_call | solution.py:497
  196.1 4.6 %all-to-all-start.4 = ((bf16[4,24,1536]{2,1,0:T(8,128)(2,1)}), bf16[4,24,1536]{2,1,0:T(8,128)(2,1)S(1)}, u32[]{:S(2)}, u32[]{:S(2)}) async-start(bf16[4,24,1536]{2,1,0:T(8,128)(2,1)} %gather_sum.2.rest_0_), calls=%async_computation.4 | async-start | bytes 589824 | tf_op jit(solution)/shard_map/all_to_all | solution.py:723
  200.7 40.7 %attend_back.1 = (bf16[1024,2304]{1,0:T(8,128)(2,1)}, bf16[768,2304]{1,0:T(8,128)(2,1)}, f32[12,8,128]{2,1,0:T(8,128)}) custom-call(bf16[1024,2304]{1,0:T(8,128)(2,1)} %multiply_convert_fusion.qkv_ref, bf16[1024,768]{1,0:T(8,128)(2,1)} %get-tuple-element.42.g_ref, bf16[12,1024,512]{2,1,0:T(8,128)(2,1)} %get-tuple-element.43.probs_ref, ...), custom_call_target="tpu_custom_call" | custom-call | flops 100000000 | bytes 100000 | tf_op jit(solution)/shard_map/attend_back/pallas_call | solution.py:316
  245.5 4.7 %collective-permute-done.3.refs_3_ = bf16[4,4,24,3200]{3,2,1,0:T(8,128)(2,1)S(1)} collective-permute-done((bf16[4,4,24,3200]{3,2,1,0:T(8,128)(2,1)S(1)}, bf16[4,4,24,3200]{3,2,1,0:T(8,128)(2,1)S(1)}, u32[]{:S(2)}, u32[]{:S(2)}) %collective-permute-start.3) | collective-permute-done | bytes 2457632 | tf_op jit(solution)/shard_map/ppermute | solution.py:715
  252.6 4.7 %all-to-all-start.5 = ((bf16[4,4,24,3200]{3,2,1,0:T(8,128)(2,1)}), bf16[4,4,24,3200]{3,2,1,0:T(8,128)(2,1)}, u32[]{:S(2)}, u32[]{:S(2)}) async-start(bf16[4,4,24,3200]{3,2,1,0:T(8,128)(2,1)} %core_part.7.refs_1_.rest_1_), calls=%async_computation.5 | async-start | bytes 4915200 | tf_op jit(solution)/shard_map/all_to_all | solution.py:719
  265.6 5.4 %last.1 = f32[1024,768]{1,0:T(8,128)S(1)} custom-call(f32[1024,768]{1,0:T(8,128)S(1)} %copy-done.1, f32[1024,768]{1,0:T(8,128)S(1)} %copy-done.12, f32[1,768]{1,0:T(1,128)S(1)} %convert_bitcast_fusion.gain_ref, bf16[768,2304]{1,0:T(8,128)(2,1)S(1)} %bitcast.53, bf16[1024,2304]{1,0:T(8,128)(2,1)S(1)} %copy-done.11, ...), custom_call_target="tpu_custom_call" | custom-call | flops 100000000 | bytes 100000 | tf_op jit(solution)/shard_map/last/pallas_call | solution.py:541
  271.0 3.8 %fusion.3.rest_1_ = bf16[1,1024,768]{2,1,0:T(8,128)(2,1)} fusion(s32[]{:T(128)S(6)} %select_n.41, bf16[1024,768]{1,0:T(8,128)(2,1)S(1)} %copy-done.22), kind=kLoop, calls=%fused_computation.17 | loop fusion | flops 3145728 | bytes 3145732 | tf_op jit(solution)/shard_map/broadcast_in_dim | solution.py:826
  276.3 12.2 %all-to-all-done.5.array_ref = bf16[4,4,24,3200]{3,2,1,0:T(8,128)(2,1)} async-done(((bf16[4,4,24,3200]{3,2,1,0:T(8,128)(2,1)}), bf16[4,4,24,3200]{3,2,1,0:T(8,128)(2,1)}, u32[]{:S(2)}, u32[]{:S(2)}) %all-to-all-start.5) | async-done | bytes 2457632 | tf_op jit(solution)/shard_map/all_to_all | solution.py:719
  293.3 4.9 %all-to-all-start.6 = ((bf16[4,24,3200]{2,1,0:T(8,128)(2,1)}), bf16[4,24,3200]{2,1,0:T(8,128)(2,1)S(1)}, u32[]{:S(2)}, u32[]{:S(2)}) async-start(bf16[4,24,3200]{2,1,0:T(8,128)(2,1)} %copy-done.13), calls=%async_computation.6 | async-start | bytes 1228800 | tf_op jit(solution)/shard_map/all_to_all | solution.py:723
  304.6 9.7 %all-to-all-done.6.refs_0_ = bf16[4,24,3200]{2,1,0:T(8,128)(2,1)S(1)} async-done(((bf16[4,24,3200]{2,1,0:T(8,128)(2,1)}), bf16[4,24,3200]{2,1,0:T(8,128)(2,1)S(1)}, u32[]{:S(2)}, u32[]{:S(2)}) %all-to-all-start.6) | async-done | bytes 614432 | tf_op jit(solution)/shard_map/all_to_all | solution.py:723
  (163 shorter events, 64.0 us)
Async XLA Ops:
  7.2 12.7 %copy-start.31 = (s32[1,1024]{1,0:T(1,128)S(1)}, s32[1,1024]{1,0:T(1,128)}, u32[]{:S(2)}) copy-start(s32[1,1024]{1,0:T(1,128)} %param.19) | copy-start | bytes 12292
  7.3 16.7 %copy-start.33 = (s32[1,1024]{1,0:T(1,128)S(1)}, s32[1,1024]{1,0:T(1,128)}, u32[]{:S(2)}) copy-start(s32[1,1024]{1,0:T(1,128)} %param.21) | copy-start | bytes 12292
  7.3 16.7 %copy-start.34 = (s32[1,1024]{1,0:T(1,128)S(1)}, s32[1,1024]{1,0:T(1,128)}, u32[]{:S(2)}) copy-start(s32[1,1024]{1,0:T(1,128)} %param.20) | copy-start | bytes 12292
  7.3 106.9 %all-gather.2.cloned.1.call-start = ((), (), s32[]{:S(2)}) async-start(), calls=%async_computation.8 | async-start | bytes 10948608 | tf_op jit(solution)/shard_map/all_gather | solution.py:777
  9.6 17.6 %copy-start.23 = (bf16[1,1024,768]{2,1,0:T(8,128)(2,1)S(1)}, bf16[1,1024,768]{2,1,0:T(8,128)(2,1)}, u32[]{:S(2)}) copy-start(bf16[1,1024,768]{2,1,0:T(8,128)(2,1)} %param.22) | copy-start | bytes 4718596
  12.2 18.7 %copy-start.17 = (bf16[24,1]{1,0:T(8,128)(2,1)}, bf16[24,1]{1,0:T(8,128)(2,1)S(1)}, u32[]{:S(2)}) copy-start(bf16[24,1]{1,0:T(8,128)(2,1)S(1)} %copy.69.gain_ref) | copy-start | bytes 148
  13.6 24.9 %all-to-all-start = ((bf16[4,24,2432]{2,1,0:T(8,128)(2,1)}), bf16[4,24,2432]{2,1,0:T(8,128)(2,1)S(1)}, u32[]{:S(2)}, u32[]{:S(2)}) async-start(bf16[4,24,2432]{2,1,0:T(8,128)(2,1)} %broadcast_in_dim.75), calls=%async_computation | async-start | bytes 933888 | tf_op jit(solution)/shard_map/all_to_all | solution.py:730
  24.0 10.8 %copy-start.26 = (s32[1024]{0:T(1024)}, s32[1024]{0:T(1024)S(1)}, u32[]{:S(2)}) copy-start(s32[1024]{0:T(1024)S(1)} %get-tuple-element.83) | copy-start | bytes 12292
  24.0 10.8 %copy-start.27 = (s32[1024]{0:T(1024)}, s32[1024]{0:T(1024)S(1)}, u32[]{:S(2)}) copy-start(s32[1024]{0:T(1024)S(1)} %get-tuple-element.84) | copy-start | bytes 12292
  40.5 8.7 %all-to-all-start.1 = ((bf16[4,4,24,128]{3,2,1,0:T(8,128)(2,1)}), bf16[4,4,24,128]{3,2,1,0:T(8,128)(2,1)S(1)}, u32[]{:S(2)}, u32[]{:S(2)}) async-start(bf16[4,4,24,128]{3,2,1,0:T(8,128)(2,1)} %broadcast_in_dim.79), calls=%async_computation.1 | async-start | bytes 196608 | tf_op jit(solution)/shard_map/all_to_all | solution.py:719
  50.6 13.3 %copy-start = (f32[1024,768]{1,0:T(8,128)S(1)}, f32[1024,768]{1,0:T(8,128)}, u32[]{:S(2)}) copy-start(f32[1024,768]{1,0:T(8,128)} %get-tuple-element.80.refs_1_.start_ref) | copy-start | bytes 9437188
  50.6 27.1 %all-to-all-start.2 = ((bf16[4,4,24,2304]{3,2,1,0:T(8,128)(2,1)}), bf16[4,4,24,2304]{3,2,1,0:T(8,128)(2,1)}, u32[]{:S(2)}, u32[]{:S(2)}) async-start(bf16[4,4,24,2304]{3,2,1,0:T(8,128)(2,1)} %broadcast_in_dim.80), calls=%async_computation.2 | async-start | bytes 3538944 | tf_op jit(solution)/shard_map/all_to_all | solution.py:719
  55.3 243.0 %reduce-scatter.2.cloned.1.call-start = ((), (), s32[]{:S(2)}) async-start(), calls=%async_computation.9 | async-start | bytes 7299072 | tf_op jit(solution)/shard_map/reduce_scatter | solution.py:802
  55.7 1.4 collective-permute-start
  77.7 3.9 %collective-permute-start.1 = (bf16[4,4,24,2304]{3,2,1,0:T(8,128)(2,1)}, bf16[4,4,24,2304]{3,2,1,0:T(8,128)(2,1)S(1)}, u32[]{:S(2)}, u32[]{:S(2)}) collective-permute-start(bf16[4,4,24,2304]{3,2,1,0:T(8,128)(2,1)} %gate.5.own_ref), channel_id=1, source_target_pairs={{0,1},{1,0},{2,3},{3,2},{4,5},{5,4},{6,7},{7,6},{8,9},{9,8},{10,11... | collective-permute-start | bytes 5308424 | tf_op jit(solution)/shard_map/ppermute | solution.py:715
  162.1 2.9 collective-permute-start.2
  166.8 27.0 %all-to-all-start.3 = ((bf16[4,4,24,1536]{3,2,1,0:T(8,128)(2,1)}), bf16[4,4,24,1536]{3,2,1,0:T(8,128)(2,1)S(1)}, u32[]{:S(2)}, u32[]{:S(2)}) async-start(bf16[4,4,24,1536]{3,2,1,0:T(8,128)(2,1)} %core_part.5.rest_0_), calls=%async_computation.3 | async-start | bytes 2359296 | tf_op jit(solution)/shard_map/all_to_all | solution.py:719
  196.1 46.3 %all-to-all-start.4 = ((bf16[4,24,1536]{2,1,0:T(8,128)(2,1)}), bf16[4,24,1536]{2,1,0:T(8,128)(2,1)S(1)}, u32[]{:S(2)}, u32[]{:S(2)}) async-start(bf16[4,24,1536]{2,1,0:T(8,128)(2,1)} %gather_sum.2.rest_0_), calls=%async_computation.4 | async-start | bytes 589824 | tf_op jit(solution)/shard_map/all_to_all | solution.py:723
  200.7 41.8 %copy-start.10 = (bf16[768,768]{1,0:T(8,128)(2,1)S(1)}, bf16[768,768]{1,0:T(8,128)(2,1)}, u32[]{:S(2)}) copy-start(bf16[768,768]{1,0:T(8,128)(2,1)} %get-tuple-element.41) | copy-start | bytes 3538948
  245.5 4.7 %collective-permute-start.3 = (bf16[4,4,24,3200]{3,2,1,0:T(8,128)(2,1)S(1)}, bf16[4,4,24,3200]{3,2,1,0:T(8,128)(2,1)S(1)}, u32[]{:S(2)}, u32[]{:S(2)}) collective-permute-start(bf16[4,4,24,3200]{3,2,1,0:T(8,128)(2,1)S(1)} %core_part.6), channel_id=1, source_target_pairs={{0,1},{1,0},{2,3},{3,2},{4,5},{5,4},{6,7},{7,6},{8,9},{9,8},{10,11... | collective-permute-start | bytes 7372808 | tf_op jit(solution)/shard_map/ppermute | solution.py:715
  252.6 35.9 %all-to-all-start.5 = ((bf16[4,4,24,3200]{3,2,1,0:T(8,128)(2,1)}), bf16[4,4,24,3200]{3,2,1,0:T(8,128)(2,1)}, u32[]{:S(2)}, u32[]{:S(2)}) async-start(bf16[4,4,24,3200]{3,2,1,0:T(8,128)(2,1)} %core_part.7.refs_1_.rest_1_), calls=%async_computation.5 | async-start | bytes 4915200 | tf_op jit(solution)/shard_map/all_to_all | solution.py:719
  276.2 16.2 %copy-start.5 = (f32[1,1024,768]{2,1,0:T(8,128)}, f32[1,1024,768]{2,1,0:T(8,128)S(1)}, u32[]{:S(2)}) copy-start(f32[1,1024,768]{2,1,0:T(8,128)S(1)} %fusion.1.rest_0_) | copy-start | bytes 9437188
  293.3 20.9 %all-to-all-start.6 = ((bf16[4,24,3200]{2,1,0:T(8,128)(2,1)}), bf16[4,24,3200]{2,1,0:T(8,128)(2,1)S(1)}, u32[]{:S(2)}, u32[]{:S(2)}) async-start(bf16[4,24,3200]{2,1,0:T(8,128)(2,1)} %copy-done.13), calls=%async_computation.6 | async-start | bytes 1228800 | tf_op jit(solution)/shard_map/all_to_all | solution.py:723
  302.4 12.6 %copy-start.18 = (bf16[24,1]{1,0:T(8,128)(2,1)S(1)}, bf16[24,1]{1,0:T(8,128)(2,1)}, u32[]{:S(2)}) copy-start(bf16[24,1]{1,0:T(8,128)(2,1)} %copy-done.17) | copy-start | bytes 148
  (28 other events, 91.1 us)
Sparse Core Ops, SparseCore 0:
  12.1 99.4 all-gather.1
  160.3 126.8 reduce-scatter.1

commit v2 on v1

--- a/solution.py
+++ b/solution.py
@@ -275,21 +275,19 @@
         return low_grads[h, block * half + down * TILE:block * half + (down + 1) * TILE, tile * TILE:(tile + 1) * TILE].astype(F32)
 
     pressed = [dot(spread[t], marks[:, t * COORDS:(t + 1) * COORDS]) for t in range(2)]
-    highs, rests = [], []
+    folded = []
     for h in range(2):
         for square in (
             (part(h, 0, 0, 0) + part(h, 0, 1, 1)) + (part(h, 1, 0, 0) + part(h, 1, 1, 1)),
             part(h, 0, 1, 0) + part(h, 1, 1, 0),
             part(h, 0, 0, 1) + part(h, 1, 0, 1),
         ):
-            high = square.astype(BF16)
-            highs.append(high)
-            rests.append((square - high.astype(F32)).astype(BF16))
-    turned = dot(jnp.concatenate(highs + rests, axis=0), flip[...])
+            folded.append(square.astype(BF16))
+    turned = dot(jnp.concatenate(folded, axis=0), flip[...])
     for h in range(2):
         squares = [item[h * COORDS:(h + 1) * COORDS] for item in pressed]
         for place in range(3 * h, 3 * h + 3):
-            squares.append(turned[place * TILE:(place + 1) * TILE] + turned[(place + 6) * TILE:(place + 7) * TILE])
+            squares.append(turned[place * TILE:(place + 1) * TILE])
         sums = [skew_sum(square) for square in squares]
         line_sums[pl.ds(pl.multiple_of((2 * step + h) * 8, 8), 8), :] = jnp.concatenate(
             sums + [jnp.zeros_like(sums[0])] * 3, axis=0

time: 326 us -> 325 us (level)
  no operation moved by 1% of the time
where the time goes in v2:
time: 325 us
  Pallas kernels  152 us (47%)
  waiting for transfers between devices  54.5 us (17%)
  local copies, waits for them, and re-layouts  37.8 us (12%)
  starting transfers between devices  33.7 us (10%)
  other arithmetic  21.9 us (7%)
  between operations  18.4 us (6%)
  matrix products  6.9 us (2%)
    pallas_call x1, Pallas kernels, feed(): pl.pallas_call(functools.partial(feed_kernel, width, parts), grid=(parts...  46 us
    pallas_call x1, Pallas kernels, attend_back(): pl.pallas_call(functools.partial(attend_back_kernel, first), grid=(count,...  39.9 us
    all_to_all x4, waiting for transfers between devices, across_plane(): lax.all_to_all(array, 'dp', 0, 0, axis_index_groups=member_groups(members...  28.9 us
    pallas_call x1, Pallas kernels, attend(): pl.pallas_call(attend_kernel, grid=(HEADS // 2,), in_specs=[pl.BlockSpec(...  24.6 us
    pallas_call x1, Pallas kernels, feed_back(): pl.pallas_call(functools.partial(feed_back_kernel, width, steps), grid=(s...  23.4 us
    unnamed x82, local copies, waits for them, and re-layouts  19 us
    all_to_all x4, starting transfers between devices, across_plane(): lax.all_to_all(array, 'dp', 0, 0, axis_index_groups=member_groups(members...  16.6 us
    ppermute x4, waiting for transfers between devices, swap_cores(): lax.ppermute(array, 'dp', [(place, place ^ 1) for place in range(members)])  11.9 us
  transfers between devices with their start and end apart: 13, of which 9 were waited for; matrix products, arithmetic and copies ran while one was open for 14% of the time, Pallas kernels for 32%

profile of v2, /device:TPU:0, one launch (start us, length us, event | category | flops | bytes accessed | tf_op | source)
XLA Modules:
  0.0 324.8 jit_solution(14782103903139819207)
XLA Ops:
  13.6 6.3 %all-to-all-start = ((bf16[4,24,2432]{2,1,0:T(8,128)(2,1)}), bf16[4,24,2432]{2,1,0:T(8,128)(2,1)S(1)}, u32[]{:S(2)}, u32[]{:S(2)}) async-start(bf16[4,24,2432]{2,1,0:T(8,128)(2,1)} %broadcast_in_dim.75), calls=%async_computation | async-start | bytes 933888 | tf_op jit(solution)/shard_map/all_to_all | solution.py:728
  27.2 3.8 %fusion.4.refs_2_.refs_1_.up_ref = bf16[1024,768]{1,0:T(8,128)(2,1)} fusion(s32[]{:T(128)S(6)} %select_n.38, bf16[1024,768]{1,0:T(8,128)(2,1)S(1)} %bitcast.65), kind=kLoop, calls=%fused_computation.18 | loop fusion | flops 3145728 | bytes 3145732 | tf_op jit(solution)/shard_map/concatenate | solution.py:693
  31.0 3.9 %multiply_reduce_fusion = (f32[1024]{0:T(1024)S(1)}, f32[1024,768]{1,0:T(8,128)}) fusion(s32[]{:T(128)S(6)} %select_n.38, bf16[1024,768]{1,0:T(8,128)(2,1)S(1)} %bitcast.66, bf16[1024,768]{1,0:T(8,128)(2,1)S(1)} %bitcast.67), kind=kLoop, calls=%fused_computation.14 | loop fusion | flops 8649728 | bytes 6295556 | tf_op jit(solution)/shard_map/reduce_sum | solution.py:783
  34.9 3.7 %all-to-all-done = bf16[4,24,2432]{2,1,0:T(8,128)(2,1)S(1)} async-done(((bf16[4,24,2432]{2,1,0:T(8,128)(2,1)}), bf16[4,24,2432]{2,1,0:T(8,128)(2,1)S(1)}, u32[]{:S(2)}, u32[]{:S(2)}) %all-to-all-start) | async-done | bytes 466976 | tf_op jit(solution)/shard_map/all_to_all | solution.py:728
  40.5 3.7 %all-to-all-start.1 = ((bf16[4,4,24,128]{3,2,1,0:T(8,128)(2,1)}), bf16[4,4,24,128]{3,2,1,0:T(8,128)(2,1)S(1)}, u32[]{:S(2)}, u32[]{:S(2)}) async-start(bf16[4,4,24,128]{3,2,1,0:T(8,128)(2,1)} %broadcast_in_dim.79), calls=%async_computation.1 | async-start | bytes 196608 | tf_op jit(solution)/shard_map/all_to_all | solution.py:717
  44.3 5.0 %all-to-all-done.1.own_ref = bf16[4,4,24,128]{3,2,1,0:T(8,128)(2,1)S(1)} async-done(((bf16[4,4,24,128]{3,2,1,0:T(8,128)(2,1)}), bf16[4,4,24,128]{3,2,1,0:T(8,128)(2,1)S(1)}, u32[]{:S(2)}, u32[]{:S(2)}) %all-to-all-start.1) | async-done | bytes 98336 | tf_op jit(solution)/shard_map/all_to_all | solution.py:717
  50.6 4.6 %all-to-all-start.2 = ((bf16[4,4,24,2304]{3,2,1,0:T(8,128)(2,1)}), bf16[4,4,24,2304]{3,2,1,0:T(8,128)(2,1)}, u32[]{:S(2)}, u32[]{:S(2)}) async-start(bf16[4,4,24,2304]{3,2,1,0:T(8,128)(2,1)} %broadcast_in_dim.80), calls=%async_computation.2 | async-start | bytes 3538944 | tf_op jit(solution)/shard_map/all_to_all | solution.py:717
  66.2 11.6 %all-to-all-done.2.refs_0_ = bf16[4,4,24,2304]{3,2,1,0:T(8,128)(2,1)} async-done(((bf16[4,4,24,2304]{3,2,1,0:T(8,128)(2,1)}), bf16[4,4,24,2304]{3,2,1,0:T(8,128)(2,1)}, u32[]{:S(2)}, u32[]{:S(2)}) %all-to-all-start.2) | async-done | bytes 1769504 | tf_op jit(solution)/shard_map/all_to_all | solution.py:717
  77.8 3.9 %collective-permute-done.1.came_ref = bf16[4,4,24,2304]{3,2,1,0:T(8,128)(2,1)S(1)} collective-permute-done((bf16[4,4,24,2304]{3,2,1,0:T(8,128)(2,1)}, bf16[4,4,24,2304]{3,2,1,0:T(8,128)(2,1)S(1)}, u32[]{:S(2)}, u32[]{:S(2)}) %collective-permute-start.1) | collective-permute-done | bytes 1769504 | tf_op jit(solution)/shard_map/ppermute | solution.py:713
  84.0 5.5 %multiply_convert_fusion.qkv_ref = bf16[1024,2304]{1,0:T(8,128)(2,1)} fusion(bf16[1024,768]{1,0:T(8,128)(2,1)S(1)} %copy-done.19, bf16[768,2304]{1,0:T(8,128)(2,1)S(1)} %bitcast.52, f32[2304]{0:T(1024)S(1)} %fusion.14), kind=kOutput, calls=%fused_computation | convolution fusion | flops 3628597248 | bytes 9839616 | tf_op jit(solution)/shard_map/dot_general | solution.py:34
  89.5 24.6 %attend.1 = (bf16[1024,768]{1,0:T(8,128)(2,1)}, bf16[12,1024,512]{2,1,0:T(8,128)(2,1)}, f32[12,1,1024]{2,1,0:T(1,128)}) custom-call(bf16[1024,2304]{1,0:T(8,128)(2,1)} %multiply_convert_fusion.qkv_ref, f32[12,8,512]{2,1,0:T(8,128)} %copy.76.refs_4_.band_ref, s32[1024,1]{1,0:T(8,128)} %copy.71.refs_3_.refs_5_.seg_ref, s32[1,1024]{1,0:T(1,128)} %bitcast.81, ...), custom_call_target="tpu_custom_call" | custom-call | flops 100000000 | bytes 100000 | tf_op jit(solution)/shard_map/attend/pallas_call | solution.py:151
  114.2 46.0 %feed.1 = (f32[1024,768]{1,0:T(8,128)}, bf16[1024,3072]{1,0:T(8,128)(2,1)}, bf16[1024,3072]{1,0:T(8,128)(2,1)}, bf16[768,4608]{1,0:T(8,128)(2,1)}, bf16[768,1536]{1,0:T(8,128)(2,1)}) custom-call(bf16[1024,768]{1,0:T(8,128)(2,1)} %get-tuple-element.35.att_ref, f32[1024,768]{1,0:T(8,128)} %get-tuple-element.80.refs_1_.start_ref, ...), custom_call_target="tpu_custom_call" | custom-call | flops 100000000 | bytes 100000 | tf_op jit(solution)/shard_map/feed/pallas_call | solution.py:408
  162.3 2.7 collective-permute-done.2.refs_1_
  166.9 3.5 %all-to-all-start.3 = ((bf16[4,4,24,1536]{3,2,1,0:T(8,128)(2,1)}), bf16[4,4,24,1536]{3,2,1,0:T(8,128)(2,1)S(1)}, u32[]{:S(2)}, u32[]{:S(2)}) async-start(bf16[4,4,24,1536]{3,2,1,0:T(8,128)(2,1)} %core_part.5.rest_0_), calls=%async_computation.3 | async-start | bytes 2359296 | tf_op jit(solution)/shard_map/all_to_all | solution.py:717
  170.4 23.4 %feed_back.1 = (bf16[1024,768]{1,0:T(8,128)(2,1)}, f32[1024,768]{1,0:T(8,128)}, bf16[1024,768]{1,0:T(8,128)(2,1)}, f32[16,1024]{1,0:T(8,128)}, bf16[768,768]{1,0:T(8,128)(2,1)}) custom-call(bf16[1024,768]{1,0:T(8,128)(2,1)} %get-tuple-element.35.att_ref, f32[1024,768]{1,0:T(8,128)} %get-tuple-element.36.middle_ref, ...), custom_call_target="tpu_custom_call" | custom-call | flops 100000000 | bytes 100000 | tf_op jit(solution)/shard_map/feed_back/pallas_call | solution.py:495
  196.2 4.7 %all-to-all-start.4 = ((bf16[4,24,1536]{2,1,0:T(8,128)(2,1)}), bf16[4,24,1536]{2,1,0:T(8,128)(2,1)S(1)}, u32[]{:S(2)}, u32[]{:S(2)}) async-start(bf16[4,24,1536]{2,1,0:T(8,128)(2,1)} %gather_sum.2.rest_0_), calls=%async_computation.4 | async-start | bytes 589824 | tf_op jit(solution)/shard_map/all_to_all | solution.py:721
  200.8 39.9 %attend_back.1 = (bf16[1024,2304]{1,0:T(8,128)(2,1)}, bf16[768,2304]{1,0:T(8,128)(2,1)}, f32[12,8,128]{2,1,0:T(8,128)}) custom-call(bf16[1024,2304]{1,0:T(8,128)(2,1)} %multiply_convert_fusion.qkv_ref, bf16[1024,768]{1,0:T(8,128)(2,1)} %get-tuple-element.42.g_ref, bf16[12,1024,512]{2,1,0:T(8,128)(2,1)} %get-tuple-element.43.probs_ref, ...), custom_call_target="tpu_custom_call" | custom-call | flops 100000000 | bytes 100000 | tf_op jit(solution)/shard_map/attend_back/pallas_call | solution.py:314
  244.5 4.7 %collective-permute-done.3.refs_3_ = bf16[4,4,24,3200]{3,2,1,0:T(8,128)(2,1)S(1)} collective-permute-done((bf16[4,4,24,3200]{3,2,1,0:T(8,128)(2,1)S(1)}, bf16[4,4,24,3200]{3,2,1,0:T(8,128)(2,1)S(1)}, u32[]{:S(2)}, u32[]{:S(2)}) %collective-permute-start.3) | collective-permute-done | bytes 2457632 | tf_op jit(solution)/shard_map/ppermute | solution.py:713
  251.6 4.7 %all-to-all-start.5 = ((bf16[4,4,24,3200]{3,2,1,0:T(8,128)(2,1)}), bf16[4,4,24,3200]{3,2,1,0:T(8,128)(2,1)}, u32[]{:S(2)}, u32[]{:S(2)}) async-start(bf16[4,4,24,3200]{3,2,1,0:T(8,128)(2,1)} %core_part.7.refs_1_.rest_1_), calls=%async_computation.5 | async-start | bytes 4915200 | tf_op jit(solution)/shard_map/all_to_all | solution.py:717
  264.5 5.4 %last.1 = f32[1024,768]{1,0:T(8,128)S(1)} custom-call(f32[1024,768]{1,0:T(8,128)S(1)} %copy-done.1, f32[1024,768]{1,0:T(8,128)S(1)} %copy-done.12, f32[1,768]{1,0:T(1,128)S(1)} %convert_bitcast_fusion.gain_ref, bf16[768,2304]{1,0:T(8,128)(2,1)S(1)} %bitcast.53, bf16[1024,2304]{1,0:T(8,128)(2,1)S(1)} %copy-done.11, ...), custom_call_target="tpu_custom_call" | custom-call | flops 100000000 | bytes 100000 | tf_op jit(solution)/shard_map/last/pallas_call | solution.py:539
  269.9 3.7 %fusion.3.rest_1_ = bf16[1,1024,768]{2,1,0:T(8,128)(2,1)} fusion(s32[]{:T(128)S(6)} %select_n.41, bf16[1024,768]{1,0:T(8,128)(2,1)S(1)} %copy-done.22), kind=kLoop, calls=%fused_computation.17 | loop fusion | flops 3145728 | bytes 3145732 | tf_op jit(solution)/shard_map/broadcast_in_dim | solution.py:824
  275.2 12.3 %all-to-all-done.5.array_ref = bf16[4,4,24,3200]{3,2,1,0:T(8,128)(2,1)} async-done(((bf16[4,4,24,3200]{3,2,1,0:T(8,128)(2,1)}), bf16[4,4,24,3200]{3,2,1,0:T(8,128)(2,1)}, u32[]{:S(2)}, u32[]{:S(2)}) %all-to-all-start.5) | async-done | bytes 2457632 | tf_op jit(solution)/shard_map/all_to_all | solution.py:717
  292.3 5.3 %all-to-all-start.6 = ((bf16[4,24,3200]{2,1,0:T(8,128)(2,1)}), bf16[4,24,3200]{2,1,0:T(8,128)(2,1)S(1)}, u32[]{:S(2)}, u32[]{:S(2)}) async-start(bf16[4,24,3200]{2,1,0:T(8,128)(2,1)} %copy-done.13), calls=%async_computation.6 | async-start | bytes 1228800 | tf_op jit(solution)/shard_map/all_to_all | solution.py:721
  304.0 9.9 %all-to-all-done.6.refs_0_ = bf16[4,24,3200]{2,1,0:T(8,128)(2,1)S(1)} async-done(((bf16[4,24,3200]{2,1,0:T(8,128)(2,1)}), bf16[4,24,3200]{2,1,0:T(8,128)(2,1)S(1)}, u32[]{:S(2)}, u32[]{:S(2)}) %all-to-all-start.6) | async-done | bytes 614432 | tf_op jit(solution)/shard_map/all_to_all | solution.py:721
  (163 shorter events, 63.6 us)
Async XLA Ops:
  7.2 12.7 %copy-start.31 = (s32[1,1024]{1,0:T(1,128)S(1)}, s32[1,1024]{1,0:T(1,128)}, u32[]{:S(2)}) copy-start(s32[1,1024]{1,0:T(1,128)} %param.19) | copy-start | bytes 12292
  7.3 16.7 %copy-start.33 = (s32[1,1024]{1,0:T(1,128)S(1)}, s32[1,1024]{1,0:T(1,128)}, u32[]{:S(2)}) copy-start(s32[1,1024]{1,0:T(1,128)} %param.21) | copy-start | bytes 12292
  7.3 16.7 %copy-start.34 = (s32[1,1024]{1,0:T(1,128)S(1)}, s32[1,1024]{1,0:T(1,128)}, u32[]{:S(2)}) copy-start(s32[1,1024]{1,0:T(1,128)} %param.20) | copy-start | bytes 12292
  7.3 106.9 %all-gather.2.cloned.1.call-start = ((), (), s32[]{:S(2)}) async-start(), calls=%async_computation.8 | async-start | bytes 10948608 | tf_op jit(solution)/shard_map/all_gather | solution.py:775
  9.6 17.6 %copy-start.23 = (bf16[1,1024,768]{2,1,0:T(8,128)(2,1)S(1)}, bf16[1,1024,768]{2,1,0:T(8,128)(2,1)}, u32[]{:S(2)}) copy-start(bf16[1,1024,768]{2,1,0:T(8,128)(2,1)} %param.22) | copy-start | bytes 4718596
  12.2 18.8 %copy-start.17 = (bf16[24,1]{1,0:T(8,128)(2,1)}, bf16[24,1]{1,0:T(8,128)(2,1)S(1)}, u32[]{:S(2)}) copy-start(bf16[24,1]{1,0:T(8,128)(2,1)S(1)} %copy.69.gain_ref) | copy-start | bytes 148
  13.6 24.9 %all-to-all-start = ((bf16[4,24,2432]{2,1,0:T(8,128)(2,1)}), bf16[4,24,2432]{2,1,0:T(8,128)(2,1)S(1)}, u32[]{:S(2)}, u32[]{:S(2)}) async-start(bf16[4,24,2432]{2,1,0:T(8,128)(2,1)} %broadcast_in_dim.75), calls=%async_computation | async-start | bytes 933888 | tf_op jit(solution)/shard_map/all_to_all | solution.py:728
  24.0 10.8 %copy-start.26 = (s32[1024]{0:T(1024)}, s32[1024]{0:T(1024)S(1)}, u32[]{:S(2)}) copy-start(s32[1024]{0:T(1024)S(1)} %get-tuple-element.83) | copy-start | bytes 12292
  24.0 10.8 %copy-start.27 = (s32[1024]{0:T(1024)}, s32[1024]{0:T(1024)S(1)}, u32[]{:S(2)}) copy-start(s32[1024]{0:T(1024)S(1)} %get-tuple-element.84) | copy-start | bytes 12292
  40.5 8.7 %all-to-all-start.1 = ((bf16[4,4,24,128]{3,2,1,0:T(8,128)(2,1)}), bf16[4,4,24,128]{3,2,1,0:T(8,128)(2,1)S(1)}, u32[]{:S(2)}, u32[]{:S(2)}) async-start(bf16[4,4,24,128]{3,2,1,0:T(8,128)(2,1)} %broadcast_in_dim.79), calls=%async_computation.1 | async-start | bytes 196608 | tf_op jit(solution)/shard_map/all_to_all | solution.py:717
  50.6 13.3 %copy-start = (f32[1024,768]{1,0:T(8,128)S(1)}, f32[1024,768]{1,0:T(8,128)}, u32[]{:S(2)}) copy-start(f32[1024,768]{1,0:T(8,128)} %get-tuple-element.80.refs_1_.start_ref) | copy-start | bytes 9437188
  50.6 27.1 %all-to-all-start.2 = ((bf16[4,4,24,2304]{3,2,1,0:T(8,128)(2,1)}), bf16[4,4,24,2304]{3,2,1,0:T(8,128)(2,1)}, u32[]{:S(2)}, u32[]{:S(2)}) async-start(bf16[4,4,24,2304]{3,2,1,0:T(8,128)(2,1)} %broadcast_in_dim.80), calls=%async_computation.2 | async-start | bytes 3538944 | tf_op jit(solution)/shard_map/all_to_all | solution.py:717
  55.3 242.4 %reduce-scatter.2.cloned.1.call-start = ((), (), s32[]{:S(2)}) async-start(), calls=%async_computation.9 | async-start | bytes 7299072 | tf_op jit(solution)/shard_map/reduce_scatter | solution.py:800
  55.7 1.4 collective-permute-start
  77.7 3.9 %collective-permute-start.1 = (bf16[4,4,24,2304]{3,2,1,0:T(8,128)(2,1)}, bf16[4,4,24,2304]{3,2,1,0:T(8,128)(2,1)S(1)}, u32[]{:S(2)}, u32[]{:S(2)}) collective-permute-start(bf16[4,4,24,2304]{3,2,1,0:T(8,128)(2,1)} %gate.5.own_ref), channel_id=1, source_target_pairs={{0,1},{1,0},{2,3},{3,2},{4,5},{5,4},{6,7},{7,6},{8,9},{9,8},{10,11... | collective-permute-start | bytes 5308424 | tf_op jit(solution)/shard_map/ppermute | solution.py:713
  162.1 2.9 collective-permute-start.2
  166.9 27.0 %all-to-all-start.3 = ((bf16[4,4,24,1536]{3,2,1,0:T(8,128)(2,1)}), bf16[4,4,24,1536]{3,2,1,0:T(8,128)(2,1)S(1)}, u32[]{:S(2)}, u32[]{:S(2)}) async-start(bf16[4,4,24,1536]{3,2,1,0:T(8,128)(2,1)} %core_part.5.rest_0_), calls=%async_computation.3 | async-start | bytes 2359296 | tf_op jit(solution)/shard_map/all_to_all | solution.py:717
  196.2 45.6 %all-to-all-start.4 = ((bf16[4,24,1536]{2,1,0:T(8,128)(2,1)}), bf16[4,24,1536]{2,1,0:T(8,128)(2,1)S(1)}, u32[]{:S(2)}, u32[]{:S(2)}) async-start(bf16[4,24,1536]{2,1,0:T(8,128)(2,1)} %gather_sum.2.rest_0_), calls=%async_computation.4 | async-start | bytes 589824 | tf_op jit(solution)/shard_map/all_to_all | solution.py:721
  200.8 41.0 %copy-start.10 = (bf16[768,768]{1,0:T(8,128)(2,1)S(1)}, bf16[768,768]{1,0:T(8,128)(2,1)}, u32[]{:S(2)}) copy-start(bf16[768,768]{1,0:T(8,128)(2,1)} %get-tuple-element.41) | copy-start | bytes 3538948
  244.4 4.7 %collective-permute-start.3 = (bf16[4,4,24,3200]{3,2,1,0:T(8,128)(2,1)S(1)}, bf16[4,4,24,3200]{3,2,1,0:T(8,128)(2,1)S(1)}, u32[]{:S(2)}, u32[]{:S(2)}) collective-permute-start(bf16[4,4,24,3200]{3,2,1,0:T(8,128)(2,1)S(1)} %core_part.6), channel_id=1, source_target_pairs={{0,1},{1,0},{2,3},{3,2},{4,5},{5,4},{6,7},{7,6},{8,9},{9,8},{10,11... | collective-permute-start | bytes 7372808 | tf_op jit(solution)/shard_map/ppermute | solution.py:713
  251.6 35.9 %all-to-all-start.5 = ((bf16[4,4,24,3200]{3,2,1,0:T(8,128)(2,1)}), bf16[4,4,24,3200]{3,2,1,0:T(8,128)(2,1)}, u32[]{:S(2)}, u32[]{:S(2)}) async-start(bf16[4,4,24,3200]{3,2,1,0:T(8,128)(2,1)} %core_part.7.refs_1_.rest_1_), calls=%async_computation.5 | async-start | bytes 4915200 | tf_op jit(solution)/shard_map/all_to_all | solution.py:717
  275.2 16.3 %copy-start.5 = (f32[1,1024,768]{2,1,0:T(8,128)}, f32[1,1024,768]{2,1,0:T(8,128)S(1)}, u32[]{:S(2)}) copy-start(f32[1,1024,768]{2,1,0:T(8,128)S(1)} %fusion.1.rest_0_) | copy-start | bytes 9437188
  292.3 21.6 %all-to-all-start.6 = ((bf16[4,24,3200]{2,1,0:T(8,128)(2,1)}), bf16[4,24,3200]{2,1,0:T(8,128)(2,1)S(1)}, u32[]{:S(2)}, u32[]{:S(2)}) async-start(bf16[4,24,3200]{2,1,0:T(8,128)(2,1)} %copy-done.13), calls=%async_computation.6 | async-start | bytes 1228800 | tf_op jit(solution)/shard_map/all_to_all | solution.py:721
  301.8 12.9 %copy-start.18 = (bf16[24,1]{1,0:T(8,128)(2,1)S(1)}, bf16[24,1]{1,0:T(8,128)(2,1)}, u32[]{:S(2)}) copy-start(bf16[24,1]{1,0:T(8,128)(2,1)} %copy-done.17) | copy-start | bytes 148
  (28 other events, 90.9 us)
Sparse Core Ops, SparseCore 0:
  12.1 99.4 all-gather.1
  160.3 126.2 reduce-scatter.1
